TPU v7x, 1024 devices: a whole 8x8x8 slice. The times are simulated.
1024 devices in a mesh: dp: 128 (over z, x, core), tensor: 8 (over y).
Axes of the slice: x: 8, y: 8, z: 8, core: 2. Of those that a mesh axis runs over, the one named last changes fastest.
Arguments:
- tokens: bfloat16 [16384, 8192], P(('dp', 'tensor')), may hold values from -6 to 6
- grad_out: bfloat16 [16384, 28672], P('dp', 'tensor'), may hold values from -0.046875 to 0.046875
- basis: bfloat16 [8192, 128], replicated, may hold values from -0.0625 to 0.0625
- weight: float32 [8192, 28672], P('dp', 'tensor'), may hold values from -0.75 to 0.75
- exp_avg: float32 [128, 28672], P('dp', 'tensor'), may hold values from -4 to 4
- exp_avg_sq: float32 [128, 28672], P('dp', 'tensor'), may hold values from 0.0001 to 0.01
Outputs:
- new_weight: float32 [8192, 28672], P('dp', 'tensor')
- new_avg: float32 [128, 28672], P('dp', 'tensor')
- new_avg_sq: float32 [128, 28672], P('dp', 'tensor')
All inputs are finite; a program needn't handle non-finite values.
Results may differ from a plain program's by a relative error of at most 0.0033.
Values may be sent and summed in bfloat16 or wider, within the bound.
No kernel may reach another device: no remote copies, remote signals or barrier semaphores. Data moves between devices by JAX's collectives and lax.ppermute only.
A program may use at most 32 MiB of HBM per device.

v0:
```python
import jax
import jax.numpy as jnp
from jax import lax
from jax.sharding import PartitionSpec as P

STEP = 10


def body(tokens, grad_out, basis, weight, exp_avg, exp_avg_sq):
    projected = jnp.dot(
        lax.all_gather(tokens, "tensor", axis=0, tiled=True),
        basis,
        preferred_element_type=jnp.float32,
    ).astype(jnp.bfloat16)
    reduced = lax.psum_scatter(
        lax.dot_general(
            projected, grad_out, (((0,), (0,)), ((), ())), preferred_element_type=jnp.float32
        ),
        "dp",
        scatter_dimension=0,
        tiled=True,
    )
    new_avg = 0.9 * exp_avg + 0.1 * reduced
    new_avg_sq = 0.999 * exp_avg_sq + 0.001 * reduced * reduced
    first_fix = 1.0 - 0.9**STEP
    second_fix = 1.0 - 0.999**STEP
    direction = (new_avg / first_fix / (jnp.sqrt(new_avg_sq / second_fix) + 1e-08)).astype(
        jnp.bfloat16
    )
    full_direction = lax.all_gather(direction, "dp", axis=0, tiled=True)
    owned_rows = weight.shape[0]
    owner = lax.axis_index("dp")
    basis_rows = lax.dynamic_slice_in_dim(basis, owner * owned_rows, owned_rows, 0)
    delta = jnp.dot(basis_rows, full_direction, preferred_element_type=jnp.float32)
    new_weight = weight - 0.5 * delta
    return (new_weight, new_avg, new_avg_sq)


def solution(mesh):
    placed = (
        P(("dp", "tensor"), None),
        P("dp", "tensor"),
        P(),
        P("dp", "tensor"),
        P("dp", "tensor"),
        P("dp", "tensor"),
    )
    return jax.shard_map(
        body,
        mesh=mesh,
        in_specs=placed,
        out_specs=(P("dp", "tensor"), P("dp", "tensor"), P("dp", "tensor")),
        check_vma=False,
    )
```

profile of v0, /device:TPU:1, one launch (start us, length us, event | category | flops | bytes accessed | tf_op | source)
XLA Modules:
  0.0 349.6 jit_solution(13102952876926657678)
XLA Ops:
  7.2 0.0 copy-start
  7.2 0.0 all-gather.3.cloned.1.call-start
  7.2 0.7 all-gather.3.cloned.1.call-update
  7.9 0.0 copy-start.2
  7.9 0.0 copy-start.3
  7.9 0.0 all-reduce.3.cloned.1.call-start
  8.0 57.5 %all-gather.3.cloned.1.call-done = bf16[128,8192]{1,0:T(8,128)(2,1)} async-done(((bf16[16,8192]{1,0:T(8,128)(2,1)}), bf16[128,8192]{1,0:T(8,128)(2,1)}) %all-gather.3.cloned.1.call-update) | async-done | bytes 2097168 | tf_op jit(solution)/shard_map/all_gather | solution.py:11
  65.5 0.0 copy-done
  65.5 4.1 %fusion.1 = f32[128,3584]{1,0:T(8,128)} fusion(bf16[128,3584]{1,0:T(8,128)(2,1)} %param.7, bf16[128,8192]{1,0:T(8,128)(2,1)} %all-gather.3.cloned.1.call-done, bf16[8192,128]{1,0:T(8,128)(2,1)S(1)} %copy-done), kind=kOutput, calls=%fused_computation.3 | convolution fusion | flops 385892352 | bytes 6946816 | tf_op jit(solution)/shard_map/dot_general | solution.py:16
  69.6 0.0 copy-start.1
  69.7 0.0 all-reduce.3.cloned.1.call-update
  69.7 1.3 dynamic-slice
  71.0 215.4 %all-reduce.3.cloned.1.call-done = f32[128,3584]{1,0:T(8,128)} async-done(((f32[128,3584]{1,0:T(8,128)}), f32[128,3584]{1,0:T(8,128)}) %all-reduce.3.cloned.1.call-update) | async-done | bytes 1835024
  286.4 0.0 copy-done.2
  286.4 0.0 copy-done.3
  286.4 2.2 convert_bitcast_fusion
  288.6 52.9 %all-gather = bf16[128,1,3584]{2,1,0:T(2,128)(2,1)S(1)} all-gather(bf16[1,1,3584]{2,1,0:T(2,128)(2,1)S(1)} %get-tuple-element.3), channel_id=1, replica_groups=mesh['dp'=128,'tensor'=8] {'dp'}, dimensions={0}, use_global_device_ids=true | all-gather | bytes 924672 | tf_op jit(solution)/shard_map/all_gather | solution.py:30
  341.5 0.0 copy-done.1
  341.5 1.2 fusion
Async XLA Ops:
  7.2 58.3 %copy-start = (bf16[8192,128]{1,0:T(8,128)(2,1)S(1)}, bf16[8192,128]{1,0:T(8,128)(2,1)}, u32[]{:S(2)}) copy-start(bf16[8192,128]{1,0:T(8,128)(2,1)} %param.8) | copy-start | bytes 6291460
  7.2 58.3 %all-gather.3.cloned.1.call-start = ((), (), s32[]{:S(2)}) async-start(), calls=%async_computation | async-start | bytes 2359296 | tf_op jit(solution)/shard_map/all_gather | solution.py:11
  7.9 278.5 %copy-start.2 = (f32[1,3584]{1,0:T(1,128)S(1)}, f32[1,3584]{1,0:T(1,128)}, u32[]{:S(2)}) copy-start(f32[1,3584]{1,0:T(1,128)} %param.10) | copy-start | bytes 43012
  7.9 278.5 %copy-start.3 = (f32[1,3584]{1,0:T(1,128)S(1)}, f32[1,3584]{1,0:T(1,128)}, u32[]{:S(2)}) copy-start(f32[1,3584]{1,0:T(1,128)} %param.11) | copy-start | bytes 43012
  7.9 278.5 %all-reduce.3.cloned.1.call-start = ((), (), s32[]{:S(2)}) async-start(), calls=%async_computation.1 | async-start | bytes 3670016
  69.6 271.9 %copy-start.1 = (f32[64,3584]{1,0:T(8,128)S(1)}, f32[64,3584]{1,0:T(8,128)}, u32[]{:S(2)}) copy-start(f32[64,3584]{1,0:T(8,128)} %param.9) | copy-start | bytes 2752516
Sparse Core Ops, SparseCore 0:
  10.7 54.7 all-gather.2
  69.8 216.5 all-reduce.2
where the time goes:
time: 350 us
  waiting for transfers between devices  274 us (78%)
  blocking collectives  52.9 us (15%)
  between operations  14.1 us (4%)
  matrix products  5.35 us (2%)
    unnamed x3, waiting for transfers between devices  216 us
    all_gather x1, waiting for transfers between devices, body(): lax.all_gather(tokens, 'tensor', axis=0, tiled=True)  57.5 us
    all_gather x1, blocking collectives, body(): full_direction = lax.all_gather(direction, 'dp', axis=0, tiled=True)  52.9 us
  transfers between devices with their start and end apart: 2, of which 2 were waited for; matrix products, arithmetic and copies ran while one was open for 0% of the time, Pallas kernels for 0%

commit v1 on v0

v1 whole, which is shorter than its diff:
```python
import jax
import jax.numpy as jnp
from jax import lax
from jax.sharding import Mesh
from jax.sharding import PartitionSpec as P

STEP = 10
CHIPS = ("z", "x")


def own_half_first(rank):
    core = lax.axis_index("core")
    row = lax.broadcasted_iota(jnp.int32, (rank, rank), 0)
    column = lax.broadcasted_iota(jnp.int32, (rank, rank), 1)
    half = rank // 2
    wanted = jnp.where(column < half, 2 * column + core, 2 * (column - half) + 1 - core)
    return (row == wanted).astype(jnp.bfloat16)


def other_core(value):
    return lax.ppermute(value, "core", [(0, 1), (1, 0)])


def body(tokens, grad_out, basis, weight, exp_avg, exp_avg_sq):
    f32, bf16 = jnp.float32, jnp.bfloat16
    rank, columns = basis.shape[1], grad_out.shape[1]
    half, lanes = rank // 2, 128
    groups = columns // lanes
    tensor = lax.axis_size("tensor")
    own_rows = tokens.shape[0]

    order = own_half_first(rank)
    projected = jnp.dot(tokens, basis, preferred_element_type=f32).astype(bf16)
    projected = jnp.dot(projected, order, preferred_element_type=f32).astype(bf16)
    projected = lax.all_to_all(
        jnp.broadcast_to(projected[None], (tensor, own_rows, rank)), "tensor", 0, 0, tiled=True
    ).reshape(tensor * own_rows, rank)
    partial = lax.dot_general(
        projected, grad_out, (((0,), (0,)), ((), ())), preferred_element_type=f32
    )
    received = other_core(partial[half:].astype(bf16))
    chip_sum = (partial[:half] + received.astype(f32)).astype(bf16)
    rows = lax.all_to_all(chip_sum.reshape(half, groups, lanes), CHIPS, 0, 0, tiled=True)
    reduced = jnp.sum(rows.astype(f32), axis=0).reshape(1, columns)

    new_avg = 0.9 * exp_avg + 0.1 * reduced
    new_avg_sq = 0.999 * exp_avg_sq + 0.001 * reduced * reduced
    first_fix = 1.0 - 0.9**STEP
    second_fix = 1.0 - 0.999**STEP
    direction = (new_avg / first_fix / (jnp.sqrt(new_avg_sq / second_fix) + 1e-08)).astype(bf16)

    own_core = lax.all_to_all(
        jnp.broadcast_to(direction.reshape(1, groups, lanes), (half, groups, lanes)),
        CHIPS, 0, 0, tiled=True,
    )
    other = other_core(own_core).reshape(half, columns)
    own_core = own_core.reshape(half, columns)
    weight_rows = weight.shape[0]
    owner = lax.axis_index(("z", "x", "core"))
    basis_rows = lax.dynamic_slice_in_dim(basis, owner * weight_rows, weight_rows, 0)
    basis_rows = jnp.dot(basis_rows, order, preferred_element_type=f32).astype(bf16)
    delta = jnp.dot(basis_rows[:, :half], own_core, preferred_element_type=f32)
    delta = delta + jnp.dot(basis_rows[:, half:], other, preferred_element_type=f32)
    return (weight - 0.5 * delta, new_avg, new_avg_sq)


def solution(mesh):
    split = Mesh(mesh.devices.reshape(8, 8, 2, 8), ("z", "x", "core", "tensor"))
    owners = ("z", "x", "core")
    shared = P(owners, "tensor")
    placed = (P(owners + ("tensor",), None), shared, P(), shared, shared, shared)
    return jax.shard_map(
        body, mesh=split, in_specs=placed, out_specs=(shared, shared, shared), check_vma=False
    )
```

time: 350 us -> 98.5 us (0.28)
  waiting for transfers between devices: 274 us -> 18.9 us
  starting transfers between devices: 0.08 us -> 24.4 us
  between operations: 14.1 us -> 0.76 us
  blocking collectives: 52.9 us -> 46.8 us
    unnamed x3 -> x0, waiting for transfers between devices: 216 us -> none
    all_gather x1 -> x0, waiting for transfers between devices: 57.5 us -> none  [body(): lax.all_gather(tokens, 'tensor', axis=0, tiled=True)]
    all_gather x1 -> x0, blocking collectives: 52.9 us -> none  [body(): full_direction = lax.all_gather(direction, 'dp', axis=0, tiled=True)]
    all_to_all x0 -> x2, blocking collectives: none -> 46.8 us  [the longest x1 32.1 us: body(): lax.all_to_all(chip_sum.reshape(half, groups, lanes), CHIPS, 0, 0, tiled=...]
    ppermute x0 -> x2, starting transfers between devices: none -> 17.7 us  [other_core(): return lax.ppermute(value, 'core', [(0, 1), (1, 0)])]
    all_to_all x0 -> x1, waiting for transfers between devices: none -> 16.4 us  [body(): lax.all_to_all(jnp.broadcast_to(direction.reshape(1, groups, lanes), (hal...]
    all_to_all x0 -> x1, starting transfers between devices: none -> 6.62 us  [body(): lax.all_to_all(jnp.broadcast_to(direction.reshape(1, groups, lanes), (hal...]
    dot_general x1, matrix products: 4.14 us -> 0.42 us  [body(): lax.dot_general(projected, grad_out, (((0,), (0,)), ((), ())), preferred_...]
  transfers between devices with their start and end apart: 2 -> 3, of which waited for: 2 -> 3; matrix products, arithmetic and copies ran while one was open for 0% -> 0% of each run, Pallas kernels for 0% -> 0%
where the time goes in v1:
time: 98.5 us; the launch traced here: 98.1 us
  blocking collectives  46.8 us (48%)
  starting transfers between devices  24.4 us (25%)
  waiting for transfers between devices  18.9 us (19%)
  matrix products  3.57 us (4%)
  local copies, waits for them, and re-layouts  2.76 us (3%)
    all_to_all x1, blocking collectives, body(): lax.all_to_all(chip_sum.reshape(half, groups, lanes), CHIPS, 0, 0, tiled=...  32.1 us
    ppermute x2, starting transfers between devices, other_core(): return lax.ppermute(value, 'core', [(0, 1), (1, 0)])  17.7 us
    all_to_all x1, waiting for transfers between devices, body(): lax.all_to_all(jnp.broadcast_to(direction.reshape(1, groups, lanes), (hal...  16.4 us
    all_to_all x1, blocking collectives, body(): lax.all_to_all(jnp.broadcast_to(projected[None], (tensor, own_rows, rank)...  14.8 us
    all_to_all x1, starting transfers between devices, body(): lax.all_to_all(jnp.broadcast_to(direction.reshape(1, groups, lanes), (hal...  6.62 us
    ppermute x2, waiting for transfers between devices, other_core(): return lax.ppermute(value, 'core', [(0, 1), (1, 0)])  2.5 us
  transfers between devices with their start and end apart: 3, of which 3 were waited for; matrix products, arithmetic and copies ran while one was open for 0% of the time, Pallas kernels for 0%

profile of v1, /device:TPU:1, one launch (start us, length us, event | category | flops | bytes accessed | tf_op | source)
XLA Modules:
  0.0 98.1 jit_solution(13003501566636564107)
XLA Ops:
  0.6 0.0 copy-start
  0.6 0.0 copy-start.2
  0.7 1.5 %copy-done = bf16[8192,128]{1,0:T(8,128)(2,1)S(1)} copy-done((bf16[8192,128]{1,0:T(8,128)(2,1)S(1)}, bf16[8192,128]{1,0:T(8,128)(2,1)}, u32[]{:S(2)}) %copy-start) | copy-done | bytes 2097176
  2.2 1.5 %convolution_convert_fusion.1 = bf16[16,128]{1,0:T(8,128)(2,1)S(1)} fusion(bf16[16,8192]{1,0:T(8,128)(2,1)} %param.6, bf16[8192,128]{1,0:T(8,128)(2,1)S(1)} %copy-done, s32[128]{0:T(128)S(1)} %get-tuple-element.6, s32[128]{0:T(128)S(1)} %get-tuple-element.7, pred[128]{0:T(512)(128)(4,1)S(1)} %iota_compare_fusion), kind=kOutput, calls=%fused_computation.4 | convolution fusion | flops 34115584 | bytes 2364544 | tf_op jit(solution)/shard_map/dot_general | solution.py:34
  3.7 14.8 %all_to_all.15 = bf16[8,16,128]{2,1,0:T(8,128)(2,1)S(1)} all-to-all(bf16[8,16,128]{2,1,0:T(8,128)(2,1)S(1)} %broadcast_in_dim.6), channel_id=1, replica_groups=mesh['z'=8,'x'=8,'core'=2,'tensor'=8] {'tensor'}, dimensions={0} | all-to-all | bytes 65536 | tf_op jit(solution)/shard_map/all_to_all | solution.py:35
  18.5 0.4 fusion.22
  19.0 0.0 copy-start.3
  19.0 0.0 copy-start.4
  19.0 11.7 %collective-permute-start = (bf16[64,3584]{1,0:T(8,128)(2,1)S(1)}, bf16[64,3584]{1,0:T(8,128)(2,1)S(1)}, u32[]{:S(2)}, u32[]{:S(2)}) collective-permute-start(bf16[64,3584]{1,0:T(8,128)(2,1)S(1)} %slice.29), channel_id=1, source_target_pairs={{0,8},{8,0},{1,9},{9,1},{2,10},{10,2},{3,11},{11,3},{4,12},{12,4},... | collective-permute-start | bytes 1376264 | tf_op jit(solution)/shard_map/ppermute | solution.py:21
  30.7 1.4 %collective-permute-done = bf16[64,3584]{1,0:T(8,128)(2,1)S(1)} collective-permute-done((bf16[64,3584]{1,0:T(8,128)(2,1)S(1)}, bf16[64,3584]{1,0:T(8,128)(2,1)S(1)}, u32[]{:S(2)}, u32[]{:S(2)}) %collective-permute-start) | collective-permute-done | bytes 458784 | tf_op jit(solution)/shard_map/ppermute | solution.py:21
  32.1 0.1 fusion.2
  32.2 0.3 reshape.61
  32.4 32.1 %all_to_all.16 = bf16[64,28,128]{2,1,0:T(8,128)(2,1)S(1)} all-to-all(bf16[64,28,128]{2,1,0:T(8,128)(2,1)S(1)} %reshape.61), channel_id=1, replica_groups=mesh['z'=8,'x'=8,'core'=2,'tensor'=8] {'z','x'}, dimensions={0} | all-to-all | bytes 917504 | tf_op jit(solution)/shard_map/all_to_all | solution.py:43
  64.5 0.1 convert_reduce_fusion
  64.6 0.0 copy-done.3
  64.6 0.7 convert_reduce_fusion.1
  65.3 0.9 broadcast_in_dim.15
  66.2 6.6 %all-to-all-start.2 = ((bf16[64,28,128]{2,1,0:T(8,128)(2,1)}), bf16[64,28,128]{2,1,0:T(8,128)(2,1)S(1)}, u32[]{:S(2)}, u32[]{:S(2)}) async-start(bf16[64,28,128]{2,1,0:T(8,128)(2,1)} %broadcast_in_dim.15), calls=%async_computation.2 | async-start | bytes 1048576 | tf_op jit(solution)/shard_map/all_to_all | solution.py:52
  72.8 16.4 %all-to-all-done.2 = bf16[64,28,128]{2,1,0:T(8,128)(2,1)S(1)} async-done(((bf16[64,28,128]{2,1,0:T(8,128)(2,1)}), bf16[64,28,128]{2,1,0:T(8,128)(2,1)S(1)}, u32[]{:S(2)}, u32[]{:S(2)}) %all-to-all-start.2) | async-done | bytes 458784 | tf_op jit(solution)/shard_map/all_to_all | solution.py:52
  89.2 6.1 %collective-permute-start.1 = (bf16[64,28,128]{2,1,0:T(8,128)(2,1)S(1)}, bf16[64,28,128]{2,1,0:T(8,128)(2,1)S(1)}, u32[]{:S(2)}, u32[]{:S(2)}) collective-permute-start(bf16[64,28,128]{2,1,0:T(8,128)(2,1)S(1)} %all-to-all-done.2), channel_id=1, source_target_pairs={{0,8},{8,0},{1,9},{9,1},{2,10},{10,2},{3,11},{11,3},{4,12},{12,4},... | collective-permute-start | bytes 1376264 | tf_op jit(solution)/shard_map/ppermute | solution.py:21
  95.3 0.1 convolution_convert_fusion
  95.4 0.3 fusion.5
  95.7 1.1 %collective-permute-done.1 = bf16[64,28,128]{2,1,0:T(8,128)(2,1)S(1)} collective-permute-done((bf16[64,28,128]{2,1,0:T(8,128)(2,1)S(1)}, bf16[64,28,128]{2,1,0:T(8,128)(2,1)S(1)}, u32[]{:S(2)}, u32[]{:S(2)}) %collective-permute-start.1) | collective-permute-done | bytes 458784 | tf_op jit(solution)/shard_map/ppermute | solution.py:21
  96.8 1.3 %fusion.1 = f32[64,3584]{1,0:T(8,128)} fusion(f32[64,3584]{1,0:T(8,128)S(1)} %copy-done.1, f32[64,3584]{1,0:T(8,128)S(1)} %fusion.5, bf16[8,8,28,128]{3,2,1,0:T(8,128)(2,1)S(1)} %bitcast.24, bf16[64,128]{1,0:T(8,128)(2,1)S(1)} %convolution_convert_fusion), kind=kOutput, calls=%fused_computation.2 | convolution fusion | flops 30048256 | bytes 3227648 | tf_op jit(solution)/shard_map/dot_general | solution.py:63
  (8 shorter events, 0.1 us)
Async XLA Ops:
  0.6 1.6 %copy-start = (bf16[8192,128]{1,0:T(8,128)(2,1)S(1)}, bf16[8192,128]{1,0:T(8,128)(2,1)}, u32[]{:S(2)}) copy-start(bf16[8192,128]{1,0:T(8,128)(2,1)} %param.8) | copy-start | bytes 6291460
  0.6 17.8 %copy-start.2 = (bf16[128,3584]{1,0:T(8,128)(2,1)S(1)}, bf16[128,3584]{1,0:T(8,128)(2,1)}, u32[]{:S(2)}) copy-start(bf16[128,3584]{1,0:T(8,128)(2,1)} %param.7) | copy-start | bytes 2752516
  19.0 45.7 %copy-start.3 = (f32[1,3584]{1,0:T(1,128)S(1)}, f32[1,3584]{1,0:T(1,128)}, u32[]{:S(2)}) copy-start(f32[1,3584]{1,0:T(1,128)} %param.10) | copy-start | bytes 43012
  19.0 45.7 %copy-start.4 = (f32[1,3584]{1,0:T(1,128)S(1)}, f32[1,3584]{1,0:T(1,128)}, u32[]{:S(2)}) copy-start(f32[1,3584]{1,0:T(1,128)} %param.11) | copy-start | bytes 43012
  19.0 13.1 %collective-permute-start = (bf16[64,3584]{1,0:T(8,128)(2,1)S(1)}, bf16[64,3584]{1,0:T(8,128)(2,1)S(1)}, u32[]{:S(2)}, u32[]{:S(2)}) collective-permute-start(bf16[64,3584]{1,0:T(8,128)(2,1)S(1)} %slice.29), channel_id=1, source_target_pairs={{0,8},{8,0},{1,9},{9,1},{2,10},{10,2},{3,11},{11,3},{4,12},{12,4},... | collective-permute-start | bytes 1376264 | tf_op jit(solution)/shard_map/ppermute | solution.py:21
  64.5 32.3 %copy-start.1 = (f32[64,3584]{1,0:T(8,128)S(1)}, f32[64,3584]{1,0:T(8,128)}, u32[]{:S(2)}) copy-start(f32[64,3584]{1,0:T(8,128)} %param.9) | copy-start | bytes 2752516
  66.2 23.0 %all-to-all-start.2 = ((bf16[64,28,128]{2,1,0:T(8,128)(2,1)}), bf16[64,28,128]{2,1,0:T(8,128)(2,1)S(1)}, u32[]{:S(2)}, u32[]{:S(2)}) async-start(bf16[64,28,128]{2,1,0:T(8,128)(2,1)} %broadcast_in_dim.15), calls=%async_computation.2 | async-start | bytes 1048576 | tf_op jit(solution)/shard_map/all_to_all | solution.py:52
  89.2 7.6 %collective-permute-start.1 = (bf16[64,28,128]{2,1,0:T(8,128)(2,1)S(1)}, bf16[64,28,128]{2,1,0:T(8,128)(2,1)S(1)}, u32[]{:S(2)}, u32[]{:S(2)}) collective-permute-start(bf16[64,28,128]{2,1,0:T(8,128)(2,1)S(1)} %all-to-all-done.2), channel_id=1, source_target_pairs={{0,8},{8,0},{1,9},{9,1},{2,10},{10,2},{3,11},{11,3},{4,12},{12,4},... | collective-permute-start | bytes 1376264 | tf_op jit(solution)/shard_map/ppermute | solution.py:21

commit v2 on v1

v2 whole, which is shorter than its diff:
```python
import jax
import jax.numpy as jnp
from jax import lax
from jax.sharding import Mesh
from jax.sharding import PartitionSpec as P

STEP = 10
CHIPS = ("z", "x")


def by_core(rank):
    row = lax.broadcasted_iota(jnp.int32, (rank, rank), 0)
    column = lax.broadcasted_iota(jnp.int32, (rank, rank), 1)
    half = rank // 2
    wanted = jnp.where(column < half, 2 * column, 2 * (column - half) + 1)
    return (row == wanted).astype(jnp.bfloat16)


def body(tokens, grad_out, basis, weight, exp_avg, exp_avg_sq):
    f32, bf16 = jnp.float32, jnp.bfloat16
    rank, columns = basis.shape[1], grad_out.shape[1]
    half = rank // 2
    piece = (4, columns // 4)
    tensor = lax.axis_size("tensor")
    own_rows, batch_rows = tokens.shape[0], grad_out.shape[0]
    core = lax.axis_index("core")

    grad_other = lax.ppermute(grad_out, "core", [(0, 1), (1, 0)])
    order = by_core(rank)
    projected = jnp.dot(tokens, basis, preferred_element_type=f32).astype(bf16)
    projected = jnp.dot(projected, order, preferred_element_type=f32).astype(bf16)
    sent = jnp.stack([projected[:, :half], projected[:, half:]])[:, None]
    sent = jnp.broadcast_to(sent, (2, tensor, own_rows, half))
    projected = lax.all_to_all(
        sent.reshape(2 * tensor, own_rows, half), ("core", "tensor"), 0, 0, tiled=True
    ).reshape(2 * batch_rows, half)
    contract = (((0,), (0,)), ((), ()))
    first = core == 0
    chip_sum = lax.dot_general(
        projected[:batch_rows], jnp.where(first, grad_out, grad_other), contract, preferred_element_type=f32
    ) + lax.dot_general(
        projected[batch_rows:], jnp.where(first, grad_other, grad_out), contract, preferred_element_type=f32
    )
    rows = lax.all_to_all(chip_sum.astype(bf16).reshape((half,) + piece), CHIPS, 0, 0, tiled=True)
    reduced = jnp.sum(rows.astype(f32), axis=0).reshape(1, columns)

    new_avg = 0.9 * exp_avg + 0.1 * reduced
    new_avg_sq = 0.999 * exp_avg_sq + 0.001 * reduced * reduced
    first_fix = 1.0 - 0.9**STEP
    second_fix = 1.0 - 0.999**STEP
    direction = (new_avg / first_fix / (jnp.sqrt(new_avg_sq / second_fix) + 1e-08)).astype(bf16)

    weight_rows = weight.shape[0]
    owner = lax.axis_index(("z", "x", "core"))
    basis_rows = lax.dynamic_slice_in_dim(basis, owner * weight_rows, weight_rows, 0)
    basis_rows = jnp.dot(basis_rows, order, preferred_element_type=f32).astype(bf16)
    direction, basis_rows = lax.optimization_barrier((direction, basis_rows))
    own_core = lax.all_to_all(
        jnp.broadcast_to(direction.reshape((1,) + piece), (half,) + piece), CHIPS, 0, 0, tiled=True
    )
    full = lax.all_gather(own_core, "core", axis=0, tiled=True).reshape(rank, columns)
    delta = jnp.dot(basis_rows, full, preferred_element_type=f32)
    return (weight - 0.5 * delta, new_avg, new_avg_sq)


def solution(mesh):
    split = Mesh(mesh.devices.reshape(8, 8, 2, 8), ("z", "x", "core", "tensor"))
    owners = ("z", "x", "core")
    shared = P(owners, "tensor")
    placed = (P(owners + ("tensor",), None), shared, P(), shared, shared, shared)
    return jax.shard_map(
        body, mesh=split, in_specs=placed, out_specs=(shared, shared, shared), check_vma=False
    )
```

time: 98.5 us -> 93.5 us (0.949)
  blocking collectives: 46.8 us -> 28 us
  starting transfers between devices: 24.4 us -> 33.8 us
  waiting for transfers between devices: 18.9 us -> 22.7 us
  matrix products: 3.57 us -> 4.74 us
    all_to_all x2 -> x1, blocking collectives: 46.8 us -> 21.2 us  [body(): lax.all_to_all(jnp.broadcast_to(direction.reshape((1,) + piece), (half,)...]
    all_to_all x1 -> x2, starting transfers between devices: 6.62 us -> 17.5 us  [the longest x1 14.1 us: body(): lax.all_to_all(chip_sum.astype(bf16).reshape((half,) + piece), CHIPS, 0,...]
    all_gather x0 -> x1, blocking collectives: none -> 6.76 us  [body(): lax.all_gather(own_core, 'core', axis=0, tiled=True).reshape(rank, columns)]
    all_to_all x1 -> x2, waiting for transfers between devices: 16.4 us -> 22.7 us  [the longest x1 15.7 us: body(): lax.all_to_all(chip_sum.astype(bf16).reshape((half,) + piece), CHIPS, 0,...]
    ppermute x2 -> x1, waiting for transfers between devices: 2.5 us -> 0.01 us  [body(): grad_other = lax.ppermute(grad_out, 'core', [(0, 1), (1, 0)])]
    ppermute x2 -> x1, starting transfers between devices: 17.7 us -> 16.3 us  [body(): grad_other = lax.ppermute(grad_out, 'core', [(0, 1), (1, 0)])]
    dot_general x3, matrix products: 1.98 us -> 3.15 us  [the longest x1 1.57 us: body(): lax.dot_general(projected[:batch_rows], jnp.where(first, grad_out, grad_o...]
  transfers between devices with their start and end apart: 3 -> 3, of which waited for: 3 -> 2; matrix products, arithmetic and copies ran while one was open for 0% -> 3% of each run, Pallas kernels for 0% -> 0%
where the time goes in v2:
time: 93.5 us; the launch traced here: 93.1 us
  starting transfers between devices  33.8 us (36%)
  blocking collectives  28 us (30%)
  waiting for transfers between devices  22.7 us (24%)
  matrix products  4.74 us (5%)
  local copies, waits for them, and re-layouts  2.11 us (2%)
  other arithmetic  0.97 us (1%)
    all_to_all x1, blocking collectives, body(): lax.all_to_all(jnp.broadcast_to(direction.reshape((1,) + piece), (half,)...  21.2 us
    ppermute x1, starting transfers between devices, body(): grad_other = lax.ppermute(grad_out, 'core', [(0, 1), (1, 0)])  16.3 us
    all_to_all x1, waiting for transfers between devices, body(): lax.all_to_all(chip_sum.astype(bf16).reshape((half,) + piece), CHIPS, 0,...  15.7 us
    all_to_all x1, starting transfers between devices, body(): lax.all_to_all(chip_sum.astype(bf16).reshape((half,) + piece), CHIPS, 0,...  14.1 us
    all_to_all x1, waiting for transfers between devices, body(): lax.all_to_all(sent.reshape(2 * tensor, own_rows, half), ('core', 'tensor...  6.94 us
    all_gather x1, blocking collectives, body(): lax.all_gather(own_core, 'core', axis=0, tiled=True).reshape(rank, columns)  6.76 us
    all_to_all x1, starting transfers between devices, body(): lax.all_to_all(sent.reshape(2 * tensor, own_rows, half), ('core', 'tensor...  3.39 us
  transfers between devices with their start and end apart: 3, of which 2 were waited for; matrix products, arithmetic and copies ran while one was open for 3% of the time, Pallas kernels for 0%

profile of v2, /device:TPU:1, one launch (start us, length us, event | category | flops | bytes accessed | tf_op | source)
XLA Modules:
  0.0 93.1 jit_solution(16136554578189717731)
XLA Ops:
  0.6 0.0 copy-start
  0.7 16.3 %collective-permute-start = (bf16[128,3584]{1,0:T(8,128)(2,1)}, bf16[128,3584]{1,0:T(8,128)(2,1)}, u32[]{:S(2)}, u32[]{:S(2)}) collective-permute-start(bf16[128,3584]{1,0:T(8,128)(2,1)} %param.7), channel_id=1, source_target_pairs={{0,8},{8,0},{1,9},{9,1},{2,10},{10,2},{3,11},{11,3},{4,12},{12,4},... | collective-permute-start | bytes 2752520 | tf_op jit(solution)/shard_map/ppermute | solution.py:28
  17.0 1.5 %convolution_convert_fusion.1 = bf16[16,128]{1,0:T(8,128)(2,1)S(1)} fusion(bf16[16,8192]{1,0:T(8,128)(2,1)} %param.6, bf16[8192,128]{1,0:T(8,128)(2,1)S(1)} %copy-done, s32[128]{0:T(128)S(1)} %get-tuple-element.15, s32[128]{0:T(128)S(1)} %get-tuple-element.14, pred[128]{0:T(512)(128)(4,1)S(1)} %iota_compare_fusion), kind=kOutput, calls=%fused_computation.5 | convolution fusion | flops 34115584 | bytes 2364544 | tf_op jit(solution)/shard_map/dot_general | solution.py:31
  18.5 0.1 slice_bitcast_fusion.1
  18.6 0.7 reshape.65
  19.3 3.4 %all-to-all-start = ((bf16[16,2,512]{2,1,0:T(2,128)(2,1)}), bf16[16,2,512]{2,1,0:T(2,128)(2,1)S(1)}, u32[]{:S(2)}, u32[]{:S(2)}) async-start(bf16[16,2,512]{2,1,0:T(2,128)(2,1)} %reshape.65), calls=%async_computation | async-start | bytes 65536 | tf_op jit(solution)/shard_map/all_to_all | solution.py:34
  22.7 6.9 %all-to-all-done = bf16[16,2,512]{2,1,0:T(2,128)(2,1)S(1)} async-done(((bf16[16,2,512]{2,1,0:T(2,128)(2,1)}), bf16[16,2,512]{2,1,0:T(2,128)(2,1)S(1)}, u32[]{:S(2)}, u32[]{:S(2)}) %all-to-all-start) | async-done | bytes 32800 | tf_op jit(solution)/shard_map/all_to_all | solution.py:34
  29.7 0.1 reshape.66
  29.8 0.4 fusion.2
  30.2 0.0 copy-start.3
  30.2 1.6 %fusion.1 = bf16[64,3584]{1,0:T(8,128)(2,1)S(1)} fusion(f32[64,3584]{1,0:T(8,128)S(1)} %fusion.2, bf16[128,64]{1,0:T(8,128)(2,1)S(1)} %bitcast.21, bf16[128,3584]{1,0:T(8,128)(2,1)S(1)} %copy-done.1, bf16[128,3584]{1,0:T(8,128)(2,1)} %collective-permute-done, pred[]{:T(512)S(6)} %eq.9), kind=kOutput, calls=%fused_computation.3 | convolution fusion | flops 59637760 | bytes 3227649 | tf_op jit(solution)/shard_map/dot_general | solution.py:39
  31.8 0.9 reshape.61
  32.7 14.1 %all-to-all-start.1 = ((bf16[64,4,896]{2,1,0:T(4,128)(2,1)}), bf16[64,4,896]{2,1,0:T(4,128)(2,1)S(1)}, u32[]{:S(2)}, u32[]{:S(2)}) async-start(bf16[64,4,896]{2,1,0:T(4,128)(2,1)} %reshape.61), calls=%async_computation.1 | async-start | bytes 917504 | tf_op jit(solution)/shard_map/all_to_all | solution.py:44
  46.8 0.1 convolution_convert_fusion
  46.9 15.7 %all-to-all-done.1 = bf16[64,4,896]{2,1,0:T(4,128)(2,1)S(1)} async-done(((bf16[64,4,896]{2,1,0:T(4,128)(2,1)}), bf16[64,4,896]{2,1,0:T(4,128)(2,1)S(1)}, u32[]{:S(2)}, u32[]{:S(2)}) %all-to-all-start.1) | async-done | bytes 458784 | tf_op jit(solution)/shard_map/all_to_all | solution.py:44
  62.6 0.2 convert_reduce_fusion
  62.9 0.7 fusion.15
  63.6 0.1 reduce
  63.6 0.1 broadcast_in_dim.15
  63.8 0.0 copy-start.2
  63.8 21.2 %all_to_all.15 = bf16[64,4,896]{2,1,0:T(4,128)(2,1)S(1)} all-to-all(bf16[64,4,896]{2,1,0:T(4,128)(2,1)S(1)} %broadcast_in_dim.15), channel_id=1, replica_groups=mesh['z'=8,'x'=8,'core'=2,'tensor'=8] {'z','x'}, dimensions={0} | all-to-all | bytes 917504 | tf_op jit(solution)/shard_map/all_to_all | solution.py:58
  85.0 6.8 %all_gather.3 = bf16[128,4,896]{2,1,0:T(4,128)(2,1)S(1)} all-gather(bf16[64,4,896]{2,1,0:T(4,128)(2,1)S(1)} %all_to_all.15), channel_id=1, replica_groups=mesh['z'=8,'x'=8,'core'=2,'tensor'=8] {'core'}, dimensions={0}, use_global_device_ids=true | all-gather | bytes 1376256 | tf_op jit(solution)/shard_map/all_gather | solution.py:61
  91.7 0.1 copy.10
  91.9 1.2 %fusion = f32[64,3584]{1,0:T(8,128)} fusion(f32[64,3584]{1,0:T(8,128)S(1)} %copy-done.2, bf16[64,128]{1,0:T(8,128)(2,1)S(1)} %convolution_convert_fusion, bf16[128,3584]{1,0:T(8,128)(2,1)S(1)} %bitcast.19), kind=kOutput, calls=%fused_computation.1 | convolution fusion | flops 59179008 | bytes 2768896 | tf_op jit(solution)/shard_map/dot_general | solution.py:62
  (15 shorter events, 0.1 us)
Async XLA Ops:
  0.6 16.4 %copy-start = (bf16[8192,128]{1,0:T(8,128)(2,1)S(1)}, bf16[8192,128]{1,0:T(8,128)(2,1)}, u32[]{:S(2)}) copy-start(bf16[8192,128]{1,0:T(8,128)(2,1)} %param.8) | copy-start | bytes 6291460
  0.6 29.2 %copy-start.1 = (bf16[128,3584]{1,0:T(8,128)(2,1)S(1)}, bf16[128,3584]{1,0:T(8,128)(2,1)}, u32[]{:S(2)}) copy-start(bf16[128,3584]{1,0:T(8,128)(2,1)} %param.7) | copy-start | bytes 2752516
  0.7 29.2 %collective-permute-start = (bf16[128,3584]{1,0:T(8,128)(2,1)}, bf16[128,3584]{1,0:T(8,128)(2,1)}, u32[]{:S(2)}, u32[]{:S(2)}) collective-permute-start(bf16[128,3584]{1,0:T(8,128)(2,1)} %param.7), channel_id=1, source_target_pairs={{0,8},{8,0},{1,9},{9,1},{2,10},{10,2},{3,11},{11,3},{4,12},{12,4},... | collective-permute-start | bytes 2752520 | tf_op jit(solution)/shard_map/ppermute | solution.py:28
  19.3 10.4 %all-to-all-start = ((bf16[16,2,512]{2,1,0:T(2,128)(2,1)}), bf16[16,2,512]{2,1,0:T(2,128)(2,1)S(1)}, u32[]{:S(2)}, u32[]{:S(2)}) async-start(bf16[16,2,512]{2,1,0:T(2,128)(2,1)} %reshape.65), calls=%async_computation | async-start | bytes 65536 | tf_op jit(solution)/shard_map/all_to_all | solution.py:34
  30.2 32.7 %copy-start.3 = (f32[1,3584]{1,0:T(1,128)S(1)}, f32[1,3584]{1,0:T(1,128)}, u32[]{:S(2)}) copy-start(f32[1,3584]{1,0:T(1,128)} %param.10) | copy-start | bytes 43012
  30.2 32.7 %copy-start.4 = (f32[1,3584]{1,0:T(1,128)S(1)}, f32[1,3584]{1,0:T(1,128)}, u32[]{:S(2)}) copy-start(f32[1,3584]{1,0:T(1,128)} %param.11) | copy-start | bytes 43012
  32.7 29.9 %all-to-all-start.1 = ((bf16[64,4,896]{2,1,0:T(4,128)(2,1)}), bf16[64,4,896]{2,1,0:T(4,128)(2,1)S(1)}, u32[]{:S(2)}, u32[]{:S(2)}) async-start(bf16[64,4,896]{2,1,0:T(4,128)(2,1)} %reshape.61), calls=%async_computation.1 | async-start | bytes 917504 | tf_op jit(solution)/shard_map/all_to_all | solution.py:44
  63.8 28.1 %copy-start.2 = (f32[64,3584]{1,0:T(8,128)S(1)}, f32[64,3584]{1,0:T(8,128)}, u32[]{:S(2)}) copy-start(f32[64,3584]{1,0:T(8,128)} %param.9) | copy-start | bytes 2752516

commit v3 on v2

v3 whole, which is shorter than its diff:
```python
import functools

import jax
import jax.numpy as jnp
from jax import lax
from jax.experimental import pallas as pl
from jax.experimental.pallas import tpu as pltpu
from jax.sharding import Mesh
from jax.sharding import PartitionSpec as P

STEP = 10
CHIPS = ("z", "x")
VMEM_LIMIT = 16 * 1024 * 1024
TILE = 512


def chip_gradient(projected_ref, pick_ref, own_ref, other_ref, sum_ref, *, core_axis):
    batch = own_ref.shape[0]
    core = lax.axis_index(core_axis)
    own = projected_ref[pl.ds(pl.multiple_of(core * batch, batch), batch), :]
    other = projected_ref[pl.ds(pl.multiple_of((1 - core) * batch, batch), batch), :]
    contract = (((0,), (0,)), ((), ()))

    def ranks(rows):
        picked = lax.dot_general(
            pick_ref[...], rows, (((0,), (1,)), ((), ())), preferred_element_type=jnp.float32
        )
        return picked.astype(jnp.bfloat16)

    own, other = ranks(own), ranks(other)
    for start in range(0, own_ref.shape[1], TILE):
        cols = pl.ds(start, TILE)
        total = jnp.dot(own, own_ref[:, cols], preferred_element_type=jnp.float32)
        total = total + jnp.dot(other, other_ref[:, cols], preferred_element_type=jnp.float32)
        sum_ref[:, cols] = total.astype(jnp.bfloat16)


def moments(rows_ref, avg_ref, sq_ref, direction_ref, new_avg_ref, new_sq_ref):
    parts, width = rows_ref.shape[1:]
    reduced = jnp.sum(rows_ref[...].astype(jnp.float32), axis=0)
    pieces = [slice(i * width, (i + 1) * width) for i in range(parts)]
    avg = jnp.concatenate([avg_ref[:, p] for p in pieces], axis=0)
    sq = jnp.concatenate([sq_ref[:, p] for p in pieces], axis=0)
    new_avg = 0.9 * avg + 0.1 * reduced
    new_sq = 0.999 * sq + 0.001 * reduced * reduced
    first_fix = 1.0 - 0.9**STEP
    second_fix = 1.0 - 0.999**STEP
    direction = new_avg / first_fix / (jnp.sqrt(new_sq / second_fix) + 1e-08)
    direction_ref[...] = jnp.broadcast_to(direction.astype(jnp.bfloat16)[None], direction_ref.shape)
    for i, p in enumerate(pieces):
        new_avg_ref[:, p] = new_avg[i : i + 1]
        new_sq_ref[:, p] = new_sq[i : i + 1]


def body(tokens, grad_out, basis, weight, exp_avg, exp_avg_sq):
    f32, bf16 = jnp.float32, jnp.bfloat16
    rank, columns = basis.shape[1], grad_out.shape[1]
    half = rank // 2
    piece = (4, columns // 4)
    tensor = lax.axis_size("tensor")
    own_rows, batch_rows = tokens.shape[0], grad_out.shape[0]
    core = lax.axis_index("core")
    vmem = pl.BlockSpec(memory_space=pltpu.VMEM)
    params = pltpu.CompilerParams(vmem_limit_bytes=VMEM_LIMIT)

    row = lax.broadcasted_iota(jnp.int32, (rank, half), 0)
    column = lax.broadcasted_iota(jnp.int32, (rank, half), 1)
    pick = (row == 2 * column + core).astype(bf16)
    even, odd = (row == 2 * column).astype(bf16), (row == 2 * column + 1).astype(bf16)
    weight_rows = weight.shape[0]
    owner = lax.axis_index(("z", "x", "core"))
    basis_rows = lax.dynamic_slice_in_dim(basis, owner * weight_rows, weight_rows, 0)
    by_core = jnp.concatenate([even, odd], axis=1)
    basis_rows = jnp.dot(basis_rows, by_core, preferred_element_type=f32).astype(bf16)

    projected = jnp.dot(tokens, basis, preferred_element_type=f32).astype(bf16)
    projected, basis_rows, pick, grad_sent = lax.optimization_barrier((projected, basis_rows, pick, grad_out))
    grad_other = lax.ppermute(grad_sent, "core", [(0, 1), (1, 0)])
    projected = lax.all_to_all(
        jnp.broadcast_to(projected[None], (2 * tensor, own_rows, rank)), ("core", "tensor"), 0, 0, tiled=True
    ).reshape(2 * batch_rows, rank)
    in_vmem = functools.partial(pltpu.with_memory_space_constraint, memory_space=pltpu.VMEM)
    chip_sum = pl.pallas_call(
        functools.partial(chip_gradient, core_axis="core"),
        out_shape=pltpu.VMEM((half, columns), bf16),
        in_specs=[vmem] * 4,
        out_specs=vmem,
        compiler_params=params,
        name="chip_gradient",
    )(in_vmem(projected), in_vmem(pick), in_vmem(grad_out), in_vmem(grad_other))
    rows = lax.all_to_all(chip_sum.reshape((half,) + piece), CHIPS, 0, 0, tiled=True)
    direction, new_avg, new_avg_sq = pl.pallas_call(
        moments,
        out_shape=[
            pltpu.VMEM((half,) + piece, bf16),
            jax.ShapeDtypeStruct(exp_avg.shape, f32),
            jax.ShapeDtypeStruct(exp_avg.shape, f32),
        ],
        in_specs=[vmem] * 3,
        out_specs=[vmem] * 3,
        compiler_params=params,
        name="moments",
    )(in_vmem(rows), in_vmem(exp_avg), in_vmem(exp_avg_sq))

    own_core = lax.all_to_all(direction, CHIPS, 0, 0, tiled=True)
    full = lax.all_gather(own_core, "core", axis=0, tiled=True).reshape(rank, columns)
    delta = jnp.dot(basis_rows, full, preferred_element_type=f32)
    return (weight - 0.5 * delta, new_avg, new_avg_sq)


def solution(mesh):
    split = Mesh(mesh.devices.reshape(8, 8, 2, 8), ("z", "x", "core", "tensor"))
    owners = ("z", "x", "core")
    shared = P(owners, "tensor")
    placed = (P(owners + ("tensor",), None), shared, P(), shared, shared, shared)
    return jax.shard_map(
        body, mesh=split, in_specs=placed, out_specs=(shared, shared, shared), check_vma=False
    )
```

time: 93.5 us -> 91 us (0.973)
  blocking collectives: 28 us -> 67.9 us
  waiting for transfers between devices: 22.7 us -> 0.01 us
  starting transfers between devices: 33.8 us -> 16.1 us
  matrix products: 4.74 us -> 2.75 us
  Pallas kernels: 0 us -> 1.4 us
    all_to_all x1 -> x3, blocking collectives: 21.2 us -> 61.2 us  [the longest x1 30.1 us: body(): lax.all_to_all(chip_sum.reshape((half,) + piece), CHIPS, 0, 0, tiled=True)]
    all_to_all x2 -> x0, waiting for transfers between devices: 22.7 us -> none  [the longest x1 15.7 us: body(): lax.all_to_all(chip_sum.astype(bf16).reshape((half,) + piece), CHIPS, 0,...]
    all_to_all x2 -> x0, starting transfers between devices: 17.5 us -> none  [the longest x1 14.1 us: body(): lax.all_to_all(chip_sum.astype(bf16).reshape((half,) + piece), CHIPS, 0,...]
    dot_general x4 -> x2, matrix products: 3.54 us -> 1.55 us  [the longest x1 1.34 us: body(): projected = jnp.dot(tokens, basis, preferred_element_type=f32).astype(bf16)]
    pallas_call x0 -> x2, Pallas kernels: none -> 1.4 us  [the longest x1 0.85 us: body(): pl.pallas_call(moments, out_shape=[pltpu.VMEM((half,) + piece, bf16), jax...]
  transfers between devices with their start and end apart: 3 -> 1, of which waited for: 2 -> 0; matrix products, arithmetic and copies ran while one was open for 3% -> 0% of each run, Pallas kernels for 0% -> 0%
where the time goes in v3:
time: 91 us; the launch traced here: 90.7 us
  blocking collectives  67.9 us (75%)
  starting transfers between devices  16.1 us (18%)
  matrix products  2.75 us (3%)
  local copies, waits for them, and re-layouts  1.74 us (2%)
  Pallas kernels  1.4 us (2%)
    all_to_all x1, blocking collectives, body(): lax.all_to_all(chip_sum.reshape((half,) + piece), CHIPS, 0, 0, tiled=True)  30.1 us
    all_to_all x1, blocking collectives, body(): own_core = lax.all_to_all(direction, CHIPS, 0, 0, tiled=True)  21.4 us
    ppermute x1, starting transfers between devices, body(): grad_other = lax.ppermute(grad_sent, 'core', [(0, 1), (1, 0)])  16.1 us
    all_to_all x1, blocking collectives, body(): lax.all_to_all(jnp.broadcast_to(projected[None], (2 * tensor, own_rows, r...  9.63 us
    all_gather x1, blocking collectives, body(): lax.all_gather(own_core, 'core', axis=0, tiled=True).reshape(rank, columns)  6.76 us
  transfers between devices with their start and end apart: 1, of which 0 were waited for; matrix products, arithmetic and copies ran while one was open for 0% of the time, Pallas kernels for 0%

profile of v3, /device:TPU:1, one launch (start us, length us, event | category | flops | bytes accessed | tf_op | source)
XLA Modules:
  0.0 90.7 jit_solution(2206261972826027005)
XLA Ops:
  0.6 0.0 copy-start
  0.6 0.0 copy-start.1
  0.7 1.5 %copy-done = bf16[8192,128]{1,0:T(8,128)(2,1)S(1)} copy-done((bf16[8192,128]{1,0:T(8,128)(2,1)S(1)}, bf16[8192,128]{1,0:T(8,128)(2,1)}, u32[]{:S(2)}) %copy-start) | copy-done | bytes 2097176
  2.2 1.3 %convolution_convert_fusion.1 = bf16[16,128]{1,0:T(8,128)(2,1)S(1)} fusion(bf16[16,8192]{1,0:T(8,128)(2,1)} %param.6, bf16[8192,128]{1,0:T(8,128)(2,1)S(1)} %copy-done), kind=kOutput, calls=%fused_computation.3 | convolution fusion | flops 33556480 | bytes 2363392 | tf_op jit(solution)/shard_map/dot_general | solution.py:76
  3.6 0.2 convolution_convert_fusion
  3.8 0.0 copy-done.1
  3.8 16.1 %collective-permute-start = (bf16[128,3584]{1,0:T(8,128)(2,1)S(1)}, bf16[128,3584]{1,0:T(8,128)(2,1)S(1)}, u32[]{:S(2)}, u32[]{:S(2)}) collective-permute-start(bf16[128,3584]{1,0:T(8,128)(2,1)S(1)} %copy-done.1), channel_id=1, source_target_pairs={{0,8},{8,0},{1,9},{9,1},{2,10},{10,2},{3,11},{11,3},{4,12},{12,4},... | collective-permute-start | bytes 2752520 | tf_op jit(solution)/shard_map/ppermute | solution.py:78
  19.9 9.6 %all_to_all.15 = bf16[16,16,128]{2,1,0:T(8,128)(2,1)S(1)} all-to-all(bf16[16,16,128]{2,1,0:T(8,128)(2,1)S(1)} %broadcast_in_dim.2), channel_id=1, replica_groups=mesh['z'=8,'x'=8,'core'=2,'tensor'=8] {'core','tensor'}, dimensions={0} | all-to-all | bytes 131072 | tf_op jit(solution)/shard_map/all_to_all | solution.py:79
  29.5 0.0 collective-permute-done.other_ref
  29.5 0.0 copy-start.2
  29.5 0.0 copy-start.3
  29.5 0.5 chip_gradient.1
  30.1 0.1 reshape.17
  30.2 30.1 %all_to_all.16.rows_ref = bf16[64,4,896]{2,1,0:T(4,128)(2,1)S(1)} all-to-all(bf16[64,4,896]{2,1,0:T(4,128)(2,1)S(1)} %reshape.17), channel_id=1, replica_groups=mesh['z'=8,'x'=8,'core'=2,'tensor'=8] {'z','x'}, dimensions={0} | all-to-all | bytes 917504 | tf_op jit(solution)/shard_map/all_to_all | solution.py:91
  60.4 0.0 copy-done.2
  60.4 0.0 copy-done.3
  60.4 0.8 moments.1
  61.2 0.0 copy-start.4
  61.2 21.4 %all_to_all.17 = bf16[64,4,896]{2,1,0:T(4,128)(2,1)S(1)} all-to-all(bf16[64,4,896]{2,1,0:T(4,128)(2,1)S(1)} %get-tuple-element.14), channel_id=1, replica_groups=mesh['z'=8,'x'=8,'core'=2,'tensor'=8] {'z','x'}, dimensions={0} | all-to-all | bytes 917504 | tf_op jit(solution)/shard_map/all_to_all | solution.py:105
  82.6 6.8 %all_gather.3 = bf16[128,4,896]{2,1,0:T(4,128)(2,1)S(1)} all-gather(bf16[64,4,896]{2,1,0:T(4,128)(2,1)S(1)} %all_to_all.17), channel_id=1, replica_groups=mesh['z'=8,'x'=8,'core'=2,'tensor'=8] {'core'}, dimensions={0}, use_global_device_ids=true | all-gather | bytes 1376256 | tf_op jit(solution)/shard_map/all_gather | solution.py:106
  89.4 0.1 copy.9
  89.5 0.0 copy-done.4
  89.5 1.2 %fusion = f32[64,3584]{1,0:T(8,128)} fusion(f32[64,3584]{1,0:T(8,128)S(1)} %copy-done.4, bf16[64,128]{1,0:T(8,128)(2,1)S(1)} %convolution_convert_fusion, bf16[128,3584]{1,0:T(8,128)(2,1)S(1)} %bitcast.9), kind=kOutput, calls=%fused_computation.1 | convolution fusion | flops 59179008 | bytes 2768896 | tf_op jit(solution)/shard_map/dot_general | solution.py:107
  (6 shorter events, 0.1 us)
Async XLA Ops:
  0.6 1.6 %copy-start = (bf16[8192,128]{1,0:T(8,128)(2,1)S(1)}, bf16[8192,128]{1,0:T(8,128)(2,1)}, u32[]{:S(2)}) copy-start(bf16[8192,128]{1,0:T(8,128)(2,1)} %param.8) | copy-start | bytes 6291460
  0.6 3.2 %copy-start.1 = (bf16[128,3584]{1,0:T(8,128)(2,1)S(1)}, bf16[128,3584]{1,0:T(8,128)(2,1)}, u32[]{:S(2)}) copy-start(bf16[128,3584]{1,0:T(8,128)(2,1)} %own_ref.1) | copy-start | bytes 2752516
  3.8 25.7 %collective-permute-start = (bf16[128,3584]{1,0:T(8,128)(2,1)S(1)}, bf16[128,3584]{1,0:T(8,128)(2,1)S(1)}, u32[]{:S(2)}, u32[]{:S(2)}) collective-permute-start(bf16[128,3584]{1,0:T(8,128)(2,1)S(1)} %copy-done.1), channel_id=1, source_target_pairs={{0,8},{8,0},{1,9},{9,1},{2,10},{10,2},{3,11},{11,3},{4,12},{12,4},... | collective-permute-start | bytes 2752520 | tf_op jit(solution)/shard_map/ppermute | solution.py:78
  29.5 30.8 %copy-start.2 = (f32[1,3584]{1,0:T(1,128)S(1)}, f32[1,3584]{1,0:T(1,128)}, u32[]{:S(2)}) copy-start(f32[1,3584]{1,0:T(1,128)} %avg_ref.1) | copy-start | bytes 43012
  29.5 30.8 %copy-start.3 = (f32[1,3584]{1,0:T(1,128)S(1)}, f32[1,3584]{1,0:T(1,128)}, u32[]{:S(2)}) copy-start(f32[1,3584]{1,0:T(1,128)} %sq_ref.1) | copy-start | bytes 43012
  61.2 28.3 %copy-start.4 = (f32[64,3584]{1,0:T(8,128)S(1)}, f32[64,3584]{1,0:T(8,128)}, u32[]{:S(2)}) copy-start(f32[64,3584]{1,0:T(8,128)} %param.9) | copy-start | bytes 2752516

commit v4 on v3

--- a/solution.py
+++ b/solution.py
@@ -12,18 +12,69 @@
 CHIPS = ("z", "x")
 VMEM_LIMIT = 16 * 1024 * 1024
 TILE = 512
+PROJECT_PIECES = 2
+OUT_PIECES = 4
 
 
-def chip_gradient(projected_ref, pick_ref, own_ref, other_ref, sum_ref, *, core_axis):
+def project(tokens_hbm, basis_hbm, sent_ref, rows_ref, tokens_ref, basis_ref, token_sems, basis_sems):
+    depth = basis_ref.shape[0] // PROJECT_PIECES
+
+    def copies(i):
+        part = pl.ds(i * depth, depth)
+        return (
+            pltpu.make_async_copy(tokens_hbm.at[:, part], tokens_ref.at[:, part], token_sems.at[i]),
+            pltpu.make_async_copy(basis_hbm.at[part, :], basis_ref.at[part, :], basis_sems.at[i]),
+        )
+
+    for i in range(PROJECT_PIECES):
+        for copy in copies(i):
+            copy.start()
+    total = jnp.zeros((tokens_ref.shape[0], basis_ref.shape[1]), jnp.float32)
+    for i in range(PROJECT_PIECES):
+        for copy in copies(i):
+            copy.wait()
+        part = pl.ds(i * depth, depth)
+        total = total + jnp.dot(
+            tokens_ref[:, part], basis_ref[part, :], preferred_element_type=jnp.float32
+        )
+    sent_ref[...] = jnp.broadcast_to(total.astype(jnp.bfloat16)[None], sent_ref.shape)
+    count, rank = rows_ref.shape
+    half = rank // 2
+    owner = lax.axis_index(("z", "x", "core"))
+    row = lax.broadcasted_iota(jnp.int32, (rank, rank), 0)
+    column = lax.broadcasted_iota(jnp.int32, (rank, rank), 1)
+    wanted = jnp.where(column < half, 2 * column, 2 * (column - half) + 1)
+    order = jnp.where(row == wanted, 1.0, 0.0).astype(jnp.bfloat16)
+    rows = basis_ref[pl.ds(pl.multiple_of(owner * count, count), count), :]
+    rows_ref[...] = jnp.dot(rows, order, preferred_element_type=jnp.float32).astype(jnp.bfloat16)
+
+
+def update(rows_ref, direction_ref, weight_ref, new_hbm, new_ref, sems):
+    width = weight_ref.shape[1] // OUT_PIECES
+    out = []
+    for i in range(OUT_PIECES):
+        cols = pl.ds(i * width, width)
+        delta = jnp.dot(rows_ref[...], direction_ref[:, cols], preferred_element_type=jnp.float32)
+        new_ref[:, cols] = weight_ref[:, cols] - 0.5 * delta
+        out.append(pltpu.make_async_copy(new_ref.at[:, cols], new_hbm.at[:, cols], sems.at[i]))
+        out[-1].start()
+    for copy in out:
+        copy.wait()
+
+
+def chip_gradient(projected_ref, own_ref, other_ref, sum_ref, *, core_axis):
     batch = own_ref.shape[0]
     core = lax.axis_index(core_axis)
     own = projected_ref[pl.ds(pl.multiple_of(core * batch, batch), batch), :]
     other = projected_ref[pl.ds(pl.multiple_of((1 - core) * batch, batch), batch), :]
-    contract = (((0,), (0,)), ((), ()))
+    rank = projected_ref.shape[1]
+    row = lax.broadcasted_iota(jnp.int32, (rank // 2, rank), 0)
+    column = lax.broadcasted_iota(jnp.int32, (rank // 2, rank), 1)
+    pick = jnp.where(column == 2 * row + core, 1.0, 0.0).astype(jnp.bfloat16)
 
     def ranks(rows):
         picked = lax.dot_general(
-            pick_ref[...], rows, (((0,), (1,)), ((), ())), preferred_element_type=jnp.float32
+            pick, rows, (((1,), (1,)), ((), ())), preferred_element_type=jnp.float32
         )
         return picked.astype(jnp.bfloat16)
 
@@ -59,35 +110,40 @@
     piece = (4, columns // 4)
     tensor = lax.axis_size("tensor")
     own_rows, batch_rows = tokens.shape[0], grad_out.shape[0]
-    core = lax.axis_index("core")
     vmem = pl.BlockSpec(memory_space=pltpu.VMEM)
     params = pltpu.CompilerParams(vmem_limit_bytes=VMEM_LIMIT)
 
-    row = lax.broadcasted_iota(jnp.int32, (rank, half), 0)
-    column = lax.broadcasted_iota(jnp.int32, (rank, half), 1)
-    pick = (row == 2 * column + core).astype(bf16)
-    even, odd = (row == 2 * column).astype(bf16), (row == 2 * column + 1).astype(bf16)
-    weight_rows = weight.shape[0]
-    owner = lax.axis_index(("z", "x", "core"))
-    basis_rows = lax.dynamic_slice_in_dim(basis, owner * weight_rows, weight_rows, 0)
-    by_core = jnp.concatenate([even, odd], axis=1)
-    basis_rows = jnp.dot(basis_rows, by_core, preferred_element_type=f32).astype(bf16)
-
-    projected = jnp.dot(tokens, basis, preferred_element_type=f32).astype(bf16)
-    projected, basis_rows, pick, grad_sent = lax.optimization_barrier((projected, basis_rows, pick, grad_out))
+    in_hbm = functools.partial(pltpu.with_memory_space_constraint, memory_space=pltpu.HBM)
+    hbm = pl.BlockSpec(memory_space=pl.ANY)
+    sent, basis_rows = pl.pallas_call(
+        project,
+        out_shape=[
+            pltpu.VMEM((2 * tensor, own_rows, rank), bf16),
+            pltpu.VMEM((weight.shape[0], rank), bf16),
+        ],
+        in_specs=[hbm] * 2,
+        out_specs=[vmem] * 2,
+        scratch_shapes=[
+            pltpu.VMEM(tokens.shape, bf16),
+            pltpu.VMEM(basis.shape, bf16),
+            pltpu.SemaphoreType.DMA((PROJECT_PIECES,)),
+            pltpu.SemaphoreType.DMA((PROJECT_PIECES,)),
+        ],
+        compiler_params=params,
+        name="project",
+    )(in_hbm(tokens), in_hbm(basis))
+    projected = lax.all_to_all(sent, ("core", "tensor"), 0, 0, tiled=True).reshape(2 * batch_rows, rank)
+    basis_rows, grad_sent = lax.optimization_barrier((basis_rows, grad_out))
     grad_other = lax.ppermute(grad_sent, "core", [(0, 1), (1, 0)])
-    projected = lax.all_to_all(
-        jnp.broadcast_to(projected[None], (2 * tensor, own_rows, rank)), ("core", "tensor"), 0, 0, tiled=True
-    ).reshape(2 * batch_rows, rank)
     in_vmem = functools.partial(pltpu.with_memory_space_constraint, memory_space=pltpu.VMEM)
     chip_sum = pl.pallas_call(
         functools.partial(chip_gradient, core_axis="core"),
         out_shape=pltpu.VMEM((half, columns), bf16),
-        in_specs=[vmem] * 4,
+        in_specs=[vmem] * 3,
         out_specs=vmem,
         compiler_params=params,
         name="chip_gradient",
-    )(in_vmem(projected), in_vmem(pick), in_vmem(grad_out), in_vmem(grad_other))
+    )(in_vmem(projected), in_vmem(grad_out), in_vmem(grad_other))
     rows = lax.all_to_all(chip_sum.reshape((half,) + piece), CHIPS, 0, 0, tiled=True)
     direction, new_avg, new_avg_sq = pl.pallas_call(
         moments,
@@ -104,8 +160,16 @@
 
     own_core = lax.all_to_all(direction, CHIPS, 0, 0, tiled=True)
     full = lax.all_gather(own_core, "core", axis=0, tiled=True).reshape(rank, columns)
-    delta = jnp.dot(basis_rows, full, preferred_element_type=f32)
-    return (weight - 0.5 * delta, new_avg, new_avg_sq)
+    new_weight = pl.pallas_call(
+        update,
+        out_shape=jax.ShapeDtypeStruct(weight.shape, f32),
+        in_specs=[vmem] * 3,
+        out_specs=hbm,
+        scratch_shapes=[pltpu.VMEM(weight.shape, f32), pltpu.SemaphoreType.DMA((OUT_PIECES,))],
+        compiler_params=params,
+        name="update",
+    )(in_vmem(basis_rows), in_vmem(full), in_vmem(weight))
+    return (new_weight, new_avg, new_avg_sq)
 
 
 def solution(mesh):

time: 91 us -> 89.9 us (0.988)
  Pallas kernels: 1.4 us -> 4.7 us
  matrix products: 2.75 us -> 0 us
  local copies, waits for them, and re-layouts: 1.74 us -> 0.22 us
    pallas_call x0 -> x2, Pallas kernels: none -> 3.31 us  [the longest x1 2.17 us: body(): pl.pallas_call(project, out_shape=[pltpu.VMEM((2 * tensor, own_rows, rank...]
    dot_general x3 -> x0, matrix products: 2.75 us -> none  [the longest x1 1.34 us: body(): projected = jnp.dot(tokens, basis, preferred_element_type=f32).astype(bf16)]
    unnamed x11 -> x9, local copies, waits for them, and re-layouts: 1.62 us -> 0.11 us
where the time goes in v4:
time: 89.9 us; the launch traced here: 89.6 us
  blocking collectives  67.9 us (76%)
  starting transfers between devices  16.1 us (18%)
  Pallas kernels  4.7 us (5%)
    all_to_all x1, blocking collectives, body(): lax.all_to_all(chip_sum.reshape((half,) + piece), CHIPS, 0, 0, tiled=True)  30.2 us
    all_to_all x1, blocking collectives, body(): own_core = lax.all_to_all(direction, CHIPS, 0, 0, tiled=True)  21.4 us
    ppermute x1, starting transfers between devices, body(): grad_other = lax.ppermute(grad_sent, 'core', [(0, 1), (1, 0)])  16.1 us
    all_to_all x1, blocking collectives, body(): lax.all_to_all(sent, ('core', 'tensor'), 0, 0, tiled=True)  9.63 us
    all_gather x1, blocking collectives, body(): lax.all_gather(own_core, 'core', axis=0, tiled=True).reshape(rank, columns)  6.76 us
    pallas_call x1, Pallas kernels, body(): pl.pallas_call(project, out_shape=[pltpu.VMEM((2 * tensor, own_rows, rank...  2.17 us
  transfers between devices with their start and end apart: 1, of which 0 were waited for; matrix products, arithmetic and copies ran while one was open for 0% of the time, Pallas kernels for 0%

profile of v4, /device:TPU:1, one launch (start us, length us, event | category | flops | bytes accessed | tf_op | source)
XLA Modules:
  0.0 89.6 jit_solution(3904989532883869714)
XLA Ops:
  0.6 0.0 copy-start
  0.6 2.2 %project.1 = (bf16[16,16,128]{2,1,0:T(8,128)(2,1)S(1)}, bf16[64,128]{1,0:T(8,128)(2,1)S(1)}) custom-call(bf16[16,8192]{1,0:T(8,128)(2,1)} %tokens_hbm.1, bf16[8192,128]{1,0:T(8,128)(2,1)} %basis_hbm.1), custom_call_target="tpu_custom_call" | custom-call | tf_op jit(solution)/shard_map/project/pallas_call | solution.py:118
  2.8 0.0 copy-done
  2.8 16.1 %collective-permute-start = (bf16[128,3584]{1,0:T(8,128)(2,1)S(1)}, bf16[128,3584]{1,0:T(8,128)(2,1)S(1)}, u32[]{:S(2)}, u32[]{:S(2)}) collective-permute-start(bf16[128,3584]{1,0:T(8,128)(2,1)S(1)} %copy-done), channel_id=1, source_target_pairs={{0,8},{8,0},{1,9},{9,1},{2,10},{10,2},{3,11},{11,3},{4,12},{12,4},... | collective-permute-start | bytes 2752520 | tf_op jit(solution)/shard_map/ppermute | solution.py:137
  18.9 9.6 %all_to_all.15 = bf16[16,16,128]{2,1,0:T(8,128)(2,1)S(1)} all-to-all(bf16[16,16,128]{2,1,0:T(8,128)(2,1)S(1)} %get-tuple-element.12), channel_id=1, replica_groups=mesh['z'=8,'x'=8,'core'=2,'tensor'=8] {'core','tensor'}, dimensions={0} | all-to-all | bytes 131072 | tf_op jit(solution)/shard_map/all_to_all | solution.py:135
  28.5 0.0 collective-permute-done.other_ref
  28.5 0.0 copy-start.2
  28.5 0.0 copy-start.3
  28.5 0.5 chip_gradient.1
  29.1 0.1 reshape.16
  29.2 30.2 %all_to_all.16.rows_ref = bf16[64,4,896]{2,1,0:T(4,128)(2,1)S(1)} all-to-all(bf16[64,4,896]{2,1,0:T(4,128)(2,1)S(1)} %reshape.16), channel_id=1, replica_groups=mesh['z'=8,'x'=8,'core'=2,'tensor'=8] {'z','x'}, dimensions={0} | all-to-all | bytes 917504 | tf_op jit(solution)/shard_map/all_to_all | solution.py:147
  59.4 0.0 copy-done.2
  59.4 0.0 copy-done.3
  59.4 0.8 moments.1
  60.2 0.0 copy-start.1
  60.2 21.4 %all_to_all.17 = bf16[64,4,896]{2,1,0:T(4,128)(2,1)S(1)} all-to-all(bf16[64,4,896]{2,1,0:T(4,128)(2,1)S(1)} %get-tuple-element.14), channel_id=1, replica_groups=mesh['z'=8,'x'=8,'core'=2,'tensor'=8] {'z','x'}, dimensions={0} | all-to-all | bytes 917504 | tf_op jit(solution)/shard_map/all_to_all | solution.py:161
  81.6 6.8 %all_gather.3 = bf16[128,4,896]{2,1,0:T(4,128)(2,1)S(1)} all-gather(bf16[64,4,896]{2,1,0:T(4,128)(2,1)S(1)} %all_to_all.17), channel_id=1, replica_groups=mesh['z'=8,'x'=8,'core'=2,'tensor'=8] {'core'}, dimensions={0}, use_global_device_ids=true | all-gather | bytes 1376256 | tf_op jit(solution)/shard_map/all_gather | solution.py:162
  88.4 0.1 copy.9
  88.5 0.0 copy-done.1
  88.5 1.1 %update.1 = f32[64,3584]{1,0:T(8,128)} custom-call(bf16[64,128]{1,0:T(8,128)(2,1)S(1)} %get-tuple-element.11.rows_ref, bf16[128,3584]{1,0:T(8,128)(2,1)S(1)} %bitcast.3, f32[64,3584]{1,0:T(8,128)S(1)} %copy-done.1), custom_call_target="tpu_custom_call" | custom-call | tf_op jit(solution)/shard_map/update/pallas_call | solution.py:163
Async XLA Ops:
  0.6 2.2 %copy-start = (bf16[128,3584]{1,0:T(8,128)(2,1)S(1)}, bf16[128,3584]{1,0:T(8,128)(2,1)}, u32[]{:S(2)}) copy-start(bf16[128,3584]{1,0:T(8,128)(2,1)} %own_ref.1) | copy-start | bytes 2752516
  2.8 25.7 %collective-permute-start = (bf16[128,3584]{1,0:T(8,128)(2,1)S(1)}, bf16[128,3584]{1,0:T(8,128)(2,1)S(1)}, u32[]{:S(2)}, u32[]{:S(2)}) collective-permute-start(bf16[128,3584]{1,0:T(8,128)(2,1)S(1)} %copy-done), channel_id=1, source_target_pairs={{0,8},{8,0},{1,9},{9,1},{2,10},{10,2},{3,11},{11,3},{4,12},{12,4},... | collective-permute-start | bytes 2752520 | tf_op jit(solution)/shard_map/ppermute | solution.py:137
  28.5 30.8 %copy-start.2 = (f32[1,3584]{1,0:T(1,128)S(1)}, f32[1,3584]{1,0:T(1,128)}, u32[]{:S(2)}) copy-start(f32[1,3584]{1,0:T(1,128)} %avg_ref.1) | copy-start | bytes 43012
  28.5 30.8 %copy-start.3 = (f32[1,3584]{1,0:T(1,128)S(1)}, f32[1,3584]{1,0:T(1,128)}, u32[]{:S(2)}) copy-start(f32[1,3584]{1,0:T(1,128)} %sq_ref.1) | copy-start | bytes 43012
  60.2 28.3 %copy-start.1 = (f32[64,3584]{1,0:T(8,128)S(1)}, f32[64,3584]{1,0:T(8,128)}, u32[]{:S(2)}) copy-start(f32[64,3584]{1,0:T(8,128)} %weight_ref.1) | copy-start | bytes 2752516

commit v5 on v4

--- a/solution.py
+++ b/solution.py
@@ -49,9 +49,16 @@
     rows_ref[...] = jnp.dot(rows, order, preferred_element_type=jnp.float32).astype(jnp.bfloat16)
 
 
-def update(rows_ref, direction_ref, weight_ref, new_hbm, new_ref, sems):
+def update(
+    rows_ref, direction_ref, weight_ref, avg_ref, sq_ref, new_hbm, avg_hbm, sq_hbm, new_ref, sems, moment_sems
+):
+    out = [
+        pltpu.make_async_copy(avg_ref, avg_hbm, moment_sems.at[0]),
+        pltpu.make_async_copy(sq_ref, sq_hbm, moment_sems.at[1]),
+    ]
+    for copy in out:
+        copy.start()
     width = weight_ref.shape[1] // OUT_PIECES
-    out = []
     for i in range(OUT_PIECES):
         cols = pl.ds(i * width, width)
         delta = jnp.dot(rows_ref[...], direction_ref[:, cols], preferred_element_type=jnp.float32)
@@ -149,8 +156,8 @@
         moments,
         out_shape=[
             pltpu.VMEM((half,) + piece, bf16),
-            jax.ShapeDtypeStruct(exp_avg.shape, f32),
-            jax.ShapeDtypeStruct(exp_avg.shape, f32),
+            pltpu.VMEM(exp_avg.shape, f32),
+            pltpu.VMEM(exp_avg.shape, f32),
         ],
         in_specs=[vmem] * 3,
         out_specs=[vmem] * 3,
@@ -160,16 +167,19 @@
 
     own_core = lax.all_to_all(direction, CHIPS, 0, 0, tiled=True)
     full = lax.all_gather(own_core, "core", axis=0, tiled=True).reshape(rank, columns)
-    new_weight = pl.pallas_call(
+    return pl.pallas_call(
         update,
-        out_shape=jax.ShapeDtypeStruct(weight.shape, f32),
-        in_specs=[vmem] * 3,
-        out_specs=hbm,
-        scratch_shapes=[pltpu.VMEM(weight.shape, f32), pltpu.SemaphoreType.DMA((OUT_PIECES,))],
+        out_shape=[jax.ShapeDtypeStruct(array.shape, f32) for array in (weight, exp_avg, exp_avg_sq)],
+        in_specs=[vmem] * 5,
+        out_specs=[hbm] * 3,
+        scratch_shapes=[
+            pltpu.VMEM(weight.shape, f32),
+            pltpu.SemaphoreType.DMA((OUT_PIECES,)),
+            pltpu.SemaphoreType.DMA((2,)),
+        ],
         compiler_params=params,
         name="update",
-    )(in_vmem(basis_rows), in_vmem(full), in_vmem(weight))
-    return (new_weight, new_avg, new_avg_sq)
+    )(in_vmem(basis_rows), in_vmem(full), in_vmem(weight), in_vmem(new_avg), in_vmem(new_avg_sq))
 
 
 def solution(mesh):

time: 89.9 us -> 89.4 us (level)
  no operation moved by 1% of the time
where the time goes in v5:
time: 89.4 us; the launch traced here: 89.1 us
  blocking collectives  68 us (76%)
  starting transfers between devices  16.1 us (18%)
  Pallas kernels  4.14 us (5%)
    all_to_all x1, blocking collectives, body(): lax.all_to_all(chip_sum.reshape((half,) + piece), CHIPS, 0, 0, tiled=True)  30.2 us
    all_to_all x1, blocking collectives, body(): own_core = lax.all_to_all(direction, CHIPS, 0, 0, tiled=True)  21.4 us
    ppermute x1, starting transfers between devices, body(): grad_other = lax.ppermute(grad_sent, 'core', [(0, 1), (1, 0)])  16.1 us
    all_to_all x1, blocking collectives, body(): lax.all_to_all(sent, ('core', 'tensor'), 0, 0, tiled=True)  9.63 us
    all_gather x1, blocking collectives, body(): lax.all_gather(own_core, 'core', axis=0, tiled=True).reshape(rank, columns)  6.76 us
    pallas_call x1, Pallas kernels, body(): pl.pallas_call(project, out_shape=[pltpu.VMEM((2 * tensor, own_rows, rank...  2.17 us
  transfers between devices with their start and end apart: 1, of which 0 were waited for; matrix products, arithmetic and copies ran while one was open for 0% of the time, Pallas kernels for 0%

profile of v5, /device:TPU:1, one launch (start us, length us, event | category | flops | bytes accessed | tf_op | source)
XLA Modules:
  0.0 89.1 jit_solution(11966366574190669112)
XLA Ops:
  0.6 0.0 copy-start.1
  0.6 2.2 %project.1 = (bf16[16,16,128]{2,1,0:T(8,128)(2,1)S(1)}, bf16[64,128]{1,0:T(8,128)(2,1)S(1)}) custom-call(bf16[16,8192]{1,0:T(8,128)(2,1)} %tokens_hbm.1, bf16[8192,128]{1,0:T(8,128)(2,1)} %basis_hbm.1), custom_call_target="tpu_custom_call" | custom-call | tf_op jit(solution)/shard_map/project/pallas_call | solution.py:125
  2.8 0.0 copy-done.1
  2.8 16.1 %collective-permute-start = (bf16[128,3584]{1,0:T(8,128)(2,1)S(1)}, bf16[128,3584]{1,0:T(8,128)(2,1)S(1)}, u32[]{:S(2)}, u32[]{:S(2)}) collective-permute-start(bf16[128,3584]{1,0:T(8,128)(2,1)S(1)} %copy-done.1), channel_id=1, source_target_pairs={{0,8},{8,0},{1,9},{9,1},{2,10},{10,2},{3,11},{11,3},{4,12},{12,4},... | collective-permute-start | bytes 2752520 | tf_op jit(solution)/shard_map/ppermute | solution.py:144
  18.9 9.6 %all_to_all.15 = bf16[16,16,128]{2,1,0:T(8,128)(2,1)S(1)} all-to-all(bf16[16,16,128]{2,1,0:T(8,128)(2,1)S(1)} %get-tuple-element.12), channel_id=1, replica_groups=mesh['z'=8,'x'=8,'core'=2,'tensor'=8] {'core','tensor'}, dimensions={0} | all-to-all | bytes 131072 | tf_op jit(solution)/shard_map/all_to_all | solution.py:142
  28.5 0.0 collective-permute-done.other_ref
  28.5 0.0 copy-start.2
  28.5 0.0 copy-start.3
  28.5 0.5 chip_gradient.1
  29.1 0.1 reshape.16
  29.2 30.2 %all_to_all.16.rows_ref = bf16[64,4,896]{2,1,0:T(4,128)(2,1)S(1)} all-to-all(bf16[64,4,896]{2,1,0:T(4,128)(2,1)S(1)} %reshape.16), channel_id=1, replica_groups=mesh['z'=8,'x'=8,'core'=2,'tensor'=8] {'z','x'}, dimensions={0} | all-to-all | bytes 917504 | tf_op jit(solution)/shard_map/all_to_all | solution.py:154
  59.4 0.0 copy-done.2
  59.4 0.0 copy-done.3
  59.4 0.3 moments.1
  59.6 0.0 copy-start
  59.7 21.4 %all_to_all.17 = bf16[64,4,896]{2,1,0:T(4,128)(2,1)S(1)} all-to-all(bf16[64,4,896]{2,1,0:T(4,128)(2,1)S(1)} %get-tuple-element.14), channel_id=1, replica_groups=mesh['z'=8,'x'=8,'core'=2,'tensor'=8] {'z','x'}, dimensions={0} | all-to-all | bytes 917504 | tf_op jit(solution)/shard_map/all_to_all | solution.py:168
  81.1 6.8 %all_gather.3 = bf16[128,4,896]{2,1,0:T(4,128)(2,1)S(1)} all-gather(bf16[64,4,896]{2,1,0:T(4,128)(2,1)S(1)} %all_to_all.17), channel_id=1, replica_groups=mesh['z'=8,'x'=8,'core'=2,'tensor'=8] {'core'}, dimensions={0}, use_global_device_ids=true | all-gather | bytes 1376256 | tf_op jit(solution)/shard_map/all_gather | solution.py:169
  87.8 0.1 copy.9
  87.9 0.0 copy-done
  87.9 1.2 %update.1 = (f32[64,3584]{1,0:T(8,128)}, f32[1,3584]{1,0:T(1,128)}, f32[1,3584]{1,0:T(1,128)}) custom-call(bf16[64,128]{1,0:T(8,128)(2,1)S(1)} %get-tuple-element.11.rows_ref, bf16[128,3584]{1,0:T(8,128)(2,1)S(1)} %bitcast.3, f32[64,3584]{1,0:T(8,128)S(1)} %copy-done, f32[1,3584]{1,0:T(1,128)S(1)} %get-tuple-element.15.avg_ref, ...), custom_call_target="tpu_custom_call" | custom-call | tf_op jit(solution)/shard_map/update/pallas_call | solution.py:170
Async XLA Ops:
  0.6 2.2 %copy-start.1 = (bf16[128,3584]{1,0:T(8,128)(2,1)S(1)}, bf16[128,3584]{1,0:T(8,128)(2,1)}, u32[]{:S(2)}) copy-start(bf16[128,3584]{1,0:T(8,128)(2,1)} %own_ref.1) | copy-start | bytes 2752516
  2.8 25.7 %collective-permute-start = (bf16[128,3584]{1,0:T(8,128)(2,1)S(1)}, bf16[128,3584]{1,0:T(8,128)(2,1)S(1)}, u32[]{:S(2)}, u32[]{:S(2)}) collective-permute-start(bf16[128,3584]{1,0:T(8,128)(2,1)S(1)} %copy-done.1), channel_id=1, source_target_pairs={{0,8},{8,0},{1,9},{9,1},{2,10},{10,2},{3,11},{11,3},{4,12},{12,4},... | collective-permute-start | bytes 2752520 | tf_op jit(solution)/shard_map/ppermute | solution.py:144
  28.5 30.8 %copy-start.2 = (f32[1,3584]{1,0:T(1,128)S(1)}, f32[1,3584]{1,0:T(1,128)}, u32[]{:S(2)}) copy-start(f32[1,3584]{1,0:T(1,128)} %avg_ref.1) | copy-start | bytes 43012
  28.5 30.8 %copy-start.3 = (f32[1,3584]{1,0:T(1,128)S(1)}, f32[1,3584]{1,0:T(1,128)}, u32[]{:S(2)}) copy-start(f32[1,3584]{1,0:T(1,128)} %sq_ref.1) | copy-start | bytes 43012
  59.6 28.3 %copy-start = (f32[64,3584]{1,0:T(8,128)S(1)}, f32[64,3584]{1,0:T(8,128)}, u32[]{:S(2)}) copy-start(f32[64,3584]{1,0:T(8,128)} %weight_ref.1) | copy-start | bytes 2752516

commit v6 on v5

--- a/solution.py
+++ b/solution.py
@@ -38,15 +38,9 @@
             tokens_ref[:, part], basis_ref[part, :], preferred_element_type=jnp.float32
         )
     sent_ref[...] = jnp.broadcast_to(total.astype(jnp.bfloat16)[None], sent_ref.shape)
-    count, rank = rows_ref.shape
-    half = rank // 2
+    count = rows_ref.shape[0]
     owner = lax.axis_index(("z", "x", "core"))
-    row = lax.broadcasted_iota(jnp.int32, (rank, rank), 0)
-    column = lax.broadcasted_iota(jnp.int32, (rank, rank), 1)
-    wanted = jnp.where(column < half, 2 * column, 2 * (column - half) + 1)
-    order = jnp.where(row == wanted, 1.0, 0.0).astype(jnp.bfloat16)
-    rows = basis_ref[pl.ds(pl.multiple_of(owner * count, count), count), :]
-    rows_ref[...] = jnp.dot(rows, order, preferred_element_type=jnp.float32).astype(jnp.bfloat16)
+    rows_ref[...] = basis_ref[pl.ds(pl.multiple_of(owner * count, count), count), :]
 
 
 def update(
@@ -125,7 +119,7 @@
     sent, basis_rows = pl.pallas_call(
         project,
         out_shape=[
-            pltpu.VMEM((2 * tensor, own_rows, rank), bf16),
+            jax.ShapeDtypeStruct((2 * tensor, own_rows, rank), bf16),
             pltpu.VMEM((weight.shape[0], rank), bf16),
         ],
         in_specs=[hbm] * 2,
@@ -140,8 +134,17 @@
         name="project",
     )(in_hbm(tokens), in_hbm(basis))
     projected = lax.all_to_all(sent, ("core", "tensor"), 0, 0, tiled=True).reshape(2 * batch_rows, rank)
-    basis_rows, grad_sent = lax.optimization_barrier((basis_rows, grad_out))
-    grad_other = lax.ppermute(grad_sent, "core", [(0, 1), (1, 0)])
+    row = lax.broadcasted_iota(jnp.int32, (half, rank), 0)
+    column = lax.broadcasted_iota(jnp.int32, (half, rank), 1)
+    order = jnp.concatenate([column == 2 * row, column == 2 * row + 1]).astype(bf16)
+    basis_rows = lax.dot_general(
+        basis_rows, order, (((1,), (1,)), ((), ())), preferred_element_type=f32
+    ).astype(bf16)
+    grad_sent = lax.optimization_barrier((sent, grad_out))[1]
+    grad_other = jnp.concatenate(
+        [lax.ppermute(part, "core", [(0, 1), (1, 0)]) for part in jnp.split(grad_sent, 2)]
+    )
+    projected, basis_rows = lax.optimization_barrier((projected, basis_rows))
     in_vmem = functools.partial(pltpu.with_memory_space_constraint, memory_space=pltpu.VMEM)
     chip_sum = pl.pallas_call(
         functools.partial(chip_gradient, core_axis="core"),

time: 89.4 us -> 88.3 us (0.988)
  blocking collectives: 68 us -> 57.5 us
  starting transfers between devices: 16.1 us -> 21.8 us
  waiting for transfers between devices: 0.01 us -> 2.51 us
    all_to_all x0 -> x1, starting transfers between devices: none -> 17.5 us  [body(): lax.all_to_all(sent, ('core', 'tensor'), 0, 0, tiled=True)]
    ppermute x1 -> x2, starting transfers between devices: 16.1 us -> 4.33 us  [body(): lax.ppermute(part, 'core', [(0, 1), (1, 0)])]
    all_to_all x1 -> x0, blocking collectives: 9.63 us -> none  [body(): lax.all_to_all(sent, ('core', 'tensor'), 0, 0, tiled=True)]
    all_to_all x0 -> x1, waiting for transfers between devices: none -> 2.51 us  [body(): lax.all_to_all(sent, ('core', 'tensor'), 0, 0, tiled=True)]
  transfers between devices with their start and end apart: 1 -> 3, of which waited for: 0 -> 1; matrix products, arithmetic and copies ran while one was open for 0% -> 0% of each run, Pallas kernels for 0% -> 0%
where the time goes in v6:
time: 88.3 us; the launch traced here: 88 us
  blocking collectives  57.5 us (65%)
  starting transfers between devices  21.8 us (25%)
  Pallas kernels  4.75 us (5%)
  waiting for transfers between devices  2.51 us (3%)
    all_to_all x1, blocking collectives, body(): lax.all_to_all(chip_sum.reshape((half,) + piece), CHIPS, 0, 0, tiled=True)  29.4 us
    all_to_all x1, blocking collectives, body(): own_core = lax.all_to_all(direction, CHIPS, 0, 0, tiled=True)  21.3 us
    all_to_all x1, starting transfers between devices, body(): lax.all_to_all(sent, ('core', 'tensor'), 0, 0, tiled=True)  17.5 us
    all_gather x1, blocking collectives, body(): lax.all_gather(own_core, 'core', axis=0, tiled=True).reshape(rank, columns)  6.89 us
    ppermute x2, starting transfers between devices, body(): lax.ppermute(part, 'core', [(0, 1), (1, 0)])  4.33 us
    pallas_call x1, Pallas kernels, body(): pl.pallas_call(project, out_shape=[jax.ShapeDtypeStruct((2 * tensor, own_...  2.78 us
    all_to_all x1, waiting for transfers between devices, body(): lax.all_to_all(sent, ('core', 'tensor'), 0, 0, tiled=True)  2.51 us
  transfers between devices with their start and end apart: 3, of which 1 were waited for; matrix products, arithmetic and copies ran while one was open for 0% of the time, Pallas kernels for 0%

profile of v6, /device:TPU:1, one launch (start us, length us, event | category | flops | bytes accessed | tf_op | source)
XLA Modules:
  0.0 88.0 jit_solution(15124742455207945306)
XLA Ops:
  0.6 0.0 copy-start
  0.6 2.8 %project.1 = (bf16[16,16,128]{2,1,0:T(8,128)(2,1)}, bf16[64,128]{1,0:T(8,128)(2,1)S(1)}) custom-call(bf16[16,8192]{1,0:T(8,128)(2,1)} %tokens_hbm.1, bf16[8192,128]{1,0:T(8,128)(2,1)} %basis_hbm.1), custom_call_target="tpu_custom_call" | custom-call | tf_op jit(solution)/shard_map/project/pallas_call | solution.py:119
  3.4 17.5 %all-to-all-start = ((bf16[16,16,128]{2,1,0:T(8,128)(2,1)}), bf16[16,16,128]{2,1,0:T(8,128)(2,1)S(1)}, u32[]{:S(2)}, u32[]{:S(2)}) async-start(bf16[16,16,128]{2,1,0:T(8,128)(2,1)} %get-tuple-element.11), calls=%async_computation | async-start | bytes 131072 | tf_op jit(solution)/shard_map/all_to_all | solution.py:136
  20.9 0.0 copy-done
  20.9 0.1 fusion.4
  21.0 2.1 %collective-permute-start = (bf16[64,3584]{1,0:T(8,128)(2,1)S(1)}, bf16[64,3584]{1,0:T(8,128)(2,1)S(1)}, u32[]{:S(2)}, u32[]{:S(2)}) collective-permute-start(bf16[64,3584]{1,0:T(8,128)(2,1)S(1)} %get-tuple-element.19), channel_id=1, source_target_pairs={{0,8},{8,0},{1,9},{9,1},{2,10},{10,2},{3,11},{11,3},{4,12},{12,4},... | collective-permute-start | bytes 1376264 | tf_op jit(solution)/shard_map/ppermute | solution.py:145
  23.1 2.2 %collective-permute-start.1 = (bf16[64,3584]{1,0:T(8,128)(2,1)S(1)}, bf16[64,3584]{1,0:T(8,128)(2,1)S(1)}, u32[]{:S(2)}, u32[]{:S(2)}) collective-permute-start(bf16[64,3584]{1,0:T(8,128)(2,1)S(1)} %get-tuple-element.20), channel_id=1, source_target_pairs={{0,8},{8,0},{1,9},{9,1},{2,10},{10,2},{3,11},{11,3},{4,12},{12,4},... | collective-permute-start | bytes 1376264 | tf_op jit(solution)/shard_map/ppermute | solution.py:145
  25.4 0.1 iota_compare_fusion
  25.5 0.1 convolution_convert_fusion.rows_ref
  25.6 2.5 %all-to-all-done = bf16[16,16,128]{2,1,0:T(8,128)(2,1)S(1)} async-done(((bf16[16,16,128]{2,1,0:T(8,128)(2,1)}), bf16[16,16,128]{2,1,0:T(8,128)(2,1)S(1)}, u32[]{:S(2)}, u32[]{:S(2)}) %all-to-all-start) | async-done | bytes 65568 | tf_op jit(solution)/shard_map/all_to_all | solution.py:136
  28.1 0.0 collective-permute-done
  28.1 0.0 collective-permute-done.1
  28.1 0.1 pad_maximum_fusion.other_ref
  28.2 0.0 copy-start.2
  28.2 0.0 copy-start.3
  28.2 0.5 chip_gradient.1
  28.7 0.1 reshape.16
  28.9 29.4 %all_to_all.15.rows_ref = bf16[64,4,896]{2,1,0:T(4,128)(2,1)S(1)} all-to-all(bf16[64,4,896]{2,1,0:T(4,128)(2,1)S(1)} %reshape.16), channel_id=1, replica_groups=mesh['z'=8,'x'=8,'core'=2,'tensor'=8] {'z','x'}, dimensions={0} | all-to-all | bytes 917504 | tf_op jit(solution)/shard_map/all_to_all | solution.py:157
  58.2 0.0 copy-done.3
  58.2 0.3 moments.1
  58.5 21.3 %all_to_all.16 = bf16[64,4,896]{2,1,0:T(4,128)(2,1)S(1)} all-to-all(bf16[64,4,896]{2,1,0:T(4,128)(2,1)S(1)} %get-tuple-element.16), channel_id=1, replica_groups=mesh['z'=8,'x'=8,'core'=2,'tensor'=8] {'z','x'}, dimensions={0} | all-to-all | bytes 917504 | tf_op jit(solution)/shard_map/all_to_all | solution.py:171
  79.8 6.9 %all_gather.3 = bf16[128,4,896]{2,1,0:T(4,128)(2,1)S(1)} all-gather(bf16[64,4,896]{2,1,0:T(4,128)(2,1)S(1)} %all_to_all.16), channel_id=1, replica_groups=mesh['z'=8,'x'=8,'core'=2,'tensor'=8] {'core'}, dimensions={0}, use_global_device_ids=true | all-gather | bytes 1376256 | tf_op jit(solution)/shard_map/all_gather | solution.py:172
  86.7 0.1 copy.9
  86.8 1.2 %update.1 = (f32[64,3584]{1,0:T(8,128)}, f32[1,3584]{1,0:T(1,128)}, f32[1,3584]{1,0:T(1,128)}) custom-call(bf16[64,128]{1,0:T(8,128)(2,1)S(1)} %convolution_convert_fusion.rows_ref, bf16[128,3584]{1,0:T(8,128)(2,1)S(1)} %bitcast.4, f32[64,3584]{1,0:T(8,128)S(1)} %copy-done.1, f32[1,3584]{1,0:T(1,128)S(1)} %get-tuple-element.17.avg_ref, ...), custom_call_target="tpu_custom_call" | custom-call | tf_op jit(solution)/shard_map/update/pallas_call | solution.py:173
  (5 shorter events, 0.0 us)
Async XLA Ops:
  0.6 20.3 %copy-start = (bf16[128,3584]{1,0:T(8,128)(2,1)S(1)}, bf16[128,3584]{1,0:T(8,128)(2,1)}, u32[]{:S(2)}) copy-start(bf16[128,3584]{1,0:T(8,128)(2,1)} %own_ref.1) | copy-start | bytes 2752516
  3.4 24.7 %all-to-all-start = ((bf16[16,16,128]{2,1,0:T(8,128)(2,1)}), bf16[16,16,128]{2,1,0:T(8,128)(2,1)S(1)}, u32[]{:S(2)}, u32[]{:S(2)}) async-start(bf16[16,16,128]{2,1,0:T(8,128)(2,1)} %get-tuple-element.11), calls=%async_computation | async-start | bytes 131072 | tf_op jit(solution)/shard_map/all_to_all | solution.py:136
  21.0 7.1 %collective-permute-start = (bf16[64,3584]{1,0:T(8,128)(2,1)S(1)}, bf16[64,3584]{1,0:T(8,128)(2,1)S(1)}, u32[]{:S(2)}, u32[]{:S(2)}) collective-permute-start(bf16[64,3584]{1,0:T(8,128)(2,1)S(1)} %get-tuple-element.19), channel_id=1, source_target_pairs={{0,8},{8,0},{1,9},{9,1},{2,10},{10,2},{3,11},{11,3},{4,12},{12,4},... | collective-permute-start | bytes 1376264 | tf_op jit(solution)/shard_map/ppermute | solution.py:145
  23.1 5.0 %collective-permute-start.1 = (bf16[64,3584]{1,0:T(8,128)(2,1)S(1)}, bf16[64,3584]{1,0:T(8,128)(2,1)S(1)}, u32[]{:S(2)}, u32[]{:S(2)}) collective-permute-start(bf16[64,3584]{1,0:T(8,128)(2,1)S(1)} %get-tuple-element.20), channel_id=1, source_target_pairs={{0,8},{8,0},{1,9},{9,1},{2,10},{10,2},{3,11},{11,3},{4,12},{12,4},... | collective-permute-start | bytes 1376264 | tf_op jit(solution)/shard_map/ppermute | solution.py:145
  28.2 30.1 %copy-start.2 = (f32[1,3584]{1,0:T(1,128)S(1)}, f32[1,3584]{1,0:T(1,128)}, u32[]{:S(2)}) copy-start(f32[1,3584]{1,0:T(1,128)} %avg_ref.1) | copy-start | bytes 43012
  28.2 30.0 %copy-start.3 = (f32[1,3584]{1,0:T(1,128)S(1)}, f32[1,3584]{1,0:T(1,128)}, u32[]{:S(2)}) copy-start(f32[1,3584]{1,0:T(1,128)} %sq_ref.1) | copy-start | bytes 43012
  79.8 7.0 %copy-start.1 = (f32[64,3584]{1,0:T(8,128)S(1)}, f32[64,3584]{1,0:T(8,128)}, u32[]{:S(2)}) copy-start(f32[64,3584]{1,0:T(8,128)} %weight_ref.1) | copy-start | bytes 2752516

commit v7 on v6

--- a/solution.py
+++ b/solution.py
@@ -63,27 +63,33 @@
         copy.wait()
 
 
-def chip_gradient(projected_ref, own_ref, other_ref, sum_ref, *, core_axis):
-    batch = own_ref.shape[0]
+def own_gradient(projected_ref, own_ref, own_sum_ref, others_ref, *, core_axis):
+    batch, part = own_ref.shape[0], others_ref.shape[2]
     core = lax.axis_index(core_axis)
-    own = projected_ref[pl.ds(pl.multiple_of(core * batch, batch), batch), :]
-    other = projected_ref[pl.ds(pl.multiple_of((1 - core) * batch, batch), batch), :]
     rank = projected_ref.shape[1]
     row = lax.broadcasted_iota(jnp.int32, (rank // 2, rank), 0)
     column = lax.broadcasted_iota(jnp.int32, (rank // 2, rank), 1)
     pick = jnp.where(column == 2 * row + core, 1.0, 0.0).astype(jnp.bfloat16)
 
-    def ranks(rows):
-        picked = lax.dot_general(
-            pick, rows, (((1,), (1,)), ((), ())), preferred_element_type=jnp.float32
-        )
+    def ranks(start, count):
+        rows = projected_ref[pl.ds(pl.multiple_of(start, count), count), :]
+        picked = lax.dot_general(pick, rows, (((1,), (1,)), ((), ())), preferred_element_type=jnp.float32)
         return picked.astype(jnp.bfloat16)
 
-    own, other = ranks(own), ranks(other)
+    own = ranks(core * batch, batch)
+    for i in range(others_ref.shape[0]):
+        others_ref[i] = ranks((1 - core) * batch + i * part, part)
     for start in range(0, own_ref.shape[1], TILE):
         cols = pl.ds(start, TILE)
-        total = jnp.dot(own, own_ref[:, cols], preferred_element_type=jnp.float32)
-        total = total + jnp.dot(other, other_ref[:, cols], preferred_element_type=jnp.float32)
+        own_sum_ref[:, cols] = jnp.dot(own, own_ref[:, cols], preferred_element_type=jnp.float32)
+
+
+def add_other(own_sum_ref, others_ref, head_ref, tail_ref, sum_ref):
+    for start in range(0, head_ref.shape[1], TILE):
+        cols = pl.ds(start, TILE)
+        total = own_sum_ref[:, cols]
+        total = total + jnp.dot(others_ref[0], head_ref[:, cols], preferred_element_type=jnp.float32)
+        total = total + jnp.dot(others_ref[1], tail_ref[:, cols], preferred_element_type=jnp.float32)
         sum_ref[:, cols] = total.astype(jnp.bfloat16)
 
 
@@ -141,19 +147,25 @@
         basis_rows, order, (((1,), (1,)), ((), ())), preferred_element_type=f32
     ).astype(bf16)
     grad_sent = lax.optimization_barrier((sent, grad_out))[1]
-    grad_other = jnp.concatenate(
-        [lax.ppermute(part, "core", [(0, 1), (1, 0)]) for part in jnp.split(grad_sent, 2)]
-    )
+    head, tail = [lax.ppermute(part, "core", [(0, 1), (1, 0)]) for part in jnp.split(grad_sent, 2)]
     projected, basis_rows = lax.optimization_barrier((projected, basis_rows))
     in_vmem = functools.partial(pltpu.with_memory_space_constraint, memory_space=pltpu.VMEM)
+    own_sum, others = pl.pallas_call(
+        functools.partial(own_gradient, core_axis="core"),
+        out_shape=[pltpu.VMEM((half, columns), f32), pltpu.VMEM((2, half, batch_rows // 2), bf16)],
+        in_specs=[vmem] * 2,
+        out_specs=[vmem] * 2,
+        compiler_params=params,
+        name="own_gradient",
+    )(in_vmem(projected), in_vmem(grad_out))
     chip_sum = pl.pallas_call(
-        functools.partial(chip_gradient, core_axis="core"),
+        add_other,
         out_shape=pltpu.VMEM((half, columns), bf16),
-        in_specs=[vmem] * 3,
+        in_specs=[vmem] * 4,
         out_specs=vmem,
         compiler_params=params,
-        name="chip_gradient",
-    )(in_vmem(projected), in_vmem(grad_out), in_vmem(grad_other))
+        name="add_other",
+    )(in_vmem(own_sum), in_vmem(others), in_vmem(head), in_vmem(tail))
     rows = lax.all_to_all(chip_sum.reshape((half,) + piece), CHIPS, 0, 0, tiled=True)
     direction, new_avg, new_avg_sq = pl.pallas_call(
         moments,

time: 88.3 us -> 88.5 us (level)
  no operation moved by 1% of the time
where the time goes in v7:
time: 88.5 us; the launch traced here: 88.2 us
  blocking collectives  57.5 us (65%)
  starting transfers between devices  21.8 us (25%)
  Pallas kernels  5 us (6%)
  waiting for transfers between devices  2.51 us (3%)
    all_to_all x1, blocking collectives, body(): lax.all_to_all(chip_sum.reshape((half,) + piece), CHIPS, 0, 0, tiled=True)  29.4 us
    all_to_all x1, blocking collectives, body(): own_core = lax.all_to_all(direction, CHIPS, 0, 0, tiled=True)  21.4 us
    all_to_all x1, starting transfers between devices, body(): lax.all_to_all(sent, ('core', 'tensor'), 0, 0, tiled=True)  17.5 us
    all_gather x1, blocking collectives, body(): lax.all_gather(own_core, 'core', axis=0, tiled=True).reshape(rank, columns)  6.76 us
    ppermute x2, starting transfers between devices, body(): lax.ppermute(part, 'core', [(0, 1), (1, 0)])  4.33 us
    pallas_call x1, Pallas kernels, body(): pl.pallas_call(project, out_shape=[jax.ShapeDtypeStruct((2 * tensor, own_...  2.78 us
    all_to_all x1, waiting for transfers between devices, body(): lax.all_to_all(sent, ('core', 'tensor'), 0, 0, tiled=True)  2.51 us
  transfers between devices with their start and end apart: 3, of which 1 were waited for; matrix products, arithmetic and copies ran while one was open for 0% of the time, Pallas kernels for 0%

profile of v7, /device:TPU:1, one launch (start us, length us, event | category | flops | bytes accessed | tf_op | source)
XLA Modules:
  0.0 88.2 jit_solution(2238200612943738554)
XLA Ops:
  0.6 0.0 copy-start
  0.6 2.8 %project.1 = (bf16[16,16,128]{2,1,0:T(8,128)(2,1)}, bf16[64,128]{1,0:T(8,128)(2,1)S(1)}) custom-call(bf16[16,8192]{1,0:T(8,128)(2,1)} %tokens_hbm.1, bf16[8192,128]{1,0:T(8,128)(2,1)} %basis_hbm.1), custom_call_target="tpu_custom_call" | custom-call | tf_op jit(solution)/shard_map/project/pallas_call | solution.py:125
  3.4 17.5 %all-to-all-start = ((bf16[16,16,128]{2,1,0:T(8,128)(2,1)}), bf16[16,16,128]{2,1,0:T(8,128)(2,1)S(1)}, u32[]{:S(2)}, u32[]{:S(2)}) async-start(bf16[16,16,128]{2,1,0:T(8,128)(2,1)} %get-tuple-element.13), calls=%async_computation | async-start | bytes 131072 | tf_op jit(solution)/shard_map/all_to_all | solution.py:142
  20.9 0.0 copy-done
  20.9 0.1 fusion.4
  21.0 2.1 %collective-permute-start.1 = (bf16[64,3584]{1,0:T(8,128)(2,1)S(1)}, bf16[64,3584]{1,0:T(8,128)(2,1)S(1)}, u32[]{:S(2)}, u32[]{:S(2)}) collective-permute-start(bf16[64,3584]{1,0:T(8,128)(2,1)S(1)} %get-tuple-element.23), channel_id=1, source_target_pairs={{0,8},{8,0},{1,9},{9,1},{2,10},{10,2},{3,11},{11,3},{4,12},{12,4},... | collective-permute-start | bytes 1376264 | tf_op jit(solution)/shard_map/ppermute | solution.py:150
  23.1 2.2 %collective-permute-start = (bf16[64,3584]{1,0:T(8,128)(2,1)S(1)}, bf16[64,3584]{1,0:T(8,128)(2,1)S(1)}, u32[]{:S(2)}, u32[]{:S(2)}) collective-permute-start(bf16[64,3584]{1,0:T(8,128)(2,1)S(1)} %get-tuple-element.24), channel_id=1, source_target_pairs={{0,8},{8,0},{1,9},{9,1},{2,10},{10,2},{3,11},{11,3},{4,12},{12,4},... | collective-permute-start | bytes 1376264 | tf_op jit(solution)/shard_map/ppermute | solution.py:150
  25.4 0.1 iota_compare_fusion
  25.5 0.1 convolution_convert_fusion.rows_ref
  25.6 2.5 %all-to-all-done = bf16[16,16,128]{2,1,0:T(8,128)(2,1)S(1)} async-done(((bf16[16,16,128]{2,1,0:T(8,128)(2,1)}), bf16[16,16,128]{2,1,0:T(8,128)(2,1)S(1)}, u32[]{:S(2)}, u32[]{:S(2)}) %all-to-all-start) | async-done | bytes 65568 | tf_op jit(solution)/shard_map/all_to_all | solution.py:142
  28.1 0.4 own_gradient.1
  28.5 0.0 copy-start.2
  28.5 0.0 copy-start.3
  28.5 0.0 collective-permute-done.1.tail_ref
  28.6 0.0 collective-permute-done.head_ref
  28.6 0.4 add_other.1
  28.9 0.1 reshape.16
  29.1 29.4 %all_to_all.15.rows_ref = bf16[64,4,896]{2,1,0:T(4,128)(2,1)S(1)} all-to-all(bf16[64,4,896]{2,1,0:T(4,128)(2,1)S(1)} %reshape.16), channel_id=1, replica_groups=mesh['z'=8,'x'=8,'core'=2,'tensor'=8] {'z','x'}, dimensions={0} | all-to-all | bytes 917504 | tf_op jit(solution)/shard_map/all_to_all | solution.py:169
  58.4 0.3 moments.1
  58.7 0.0 copy-start.1
  58.7 21.4 %all_to_all.16 = bf16[64,4,896]{2,1,0:T(4,128)(2,1)S(1)} all-to-all(bf16[64,4,896]{2,1,0:T(4,128)(2,1)S(1)} %get-tuple-element.20), channel_id=1, replica_groups=mesh['z'=8,'x'=8,'core'=2,'tensor'=8] {'z','x'}, dimensions={0} | all-to-all | bytes 917504 | tf_op jit(solution)/shard_map/all_to_all | solution.py:183
  80.1 6.8 %all_gather.3 = bf16[128,4,896]{2,1,0:T(4,128)(2,1)S(1)} all-gather(bf16[64,4,896]{2,1,0:T(4,128)(2,1)S(1)} %all_to_all.16), channel_id=1, replica_groups=mesh['z'=8,'x'=8,'core'=2,'tensor'=8] {'core'}, dimensions={0}, use_global_device_ids=true | all-gather | bytes 1376256 | tf_op jit(solution)/shard_map/all_gather | solution.py:184
  86.9 0.1 copy.9
  87.0 1.2 %update.1 = (f32[64,3584]{1,0:T(8,128)}, f32[1,3584]{1,0:T(1,128)}, f32[1,3584]{1,0:T(1,128)}) custom-call(bf16[64,128]{1,0:T(8,128)(2,1)S(1)} %convolution_convert_fusion.rows_ref, bf16[128,3584]{1,0:T(8,128)(2,1)S(1)} %bitcast.4, f32[64,3584]{1,0:T(8,128)S(1)} %copy-done.1, f32[1,3584]{1,0:T(1,128)S(1)} %get-tuple-element.21.avg_ref, ...), custom_call_target="tpu_custom_call" | custom-call | tf_op jit(solution)/shard_map/update/pallas_call | solution.py:185
  (5 shorter events, 0.0 us)
Async XLA Ops:
  0.6 20.3 %copy-start = (bf16[128,3584]{1,0:T(8,128)(2,1)S(1)}, bf16[128,3584]{1,0:T(8,128)(2,1)}, u32[]{:S(2)}) copy-start(bf16[128,3584]{1,0:T(8,128)(2,1)} %own_ref.1) | copy-start | bytes 2752516
  3.4 24.7 %all-to-all-start = ((bf16[16,16,128]{2,1,0:T(8,128)(2,1)}), bf16[16,16,128]{2,1,0:T(8,128)(2,1)S(1)}, u32[]{:S(2)}, u32[]{:S(2)}) async-start(bf16[16,16,128]{2,1,0:T(8,128)(2,1)} %get-tuple-element.13), calls=%async_computation | async-start | bytes 131072 | tf_op jit(solution)/shard_map/all_to_all | solution.py:142
  21.0 7.5 %collective-permute-start.1 = (bf16[64,3584]{1,0:T(8,128)(2,1)S(1)}, bf16[64,3584]{1,0:T(8,128)(2,1)S(1)}, u32[]{:S(2)}, u32[]{:S(2)}) collective-permute-start(bf16[64,3584]{1,0:T(8,128)(2,1)S(1)} %get-tuple-element.23), channel_id=1, source_target_pairs={{0,8},{8,0},{1,9},{9,1},{2,10},{10,2},{3,11},{11,3},{4,12},{12,4},... | collective-permute-start | bytes 1376264 | tf_op jit(solution)/shard_map/ppermute | solution.py:150
  23.1 5.5 %collective-permute-start = (bf16[64,3584]{1,0:T(8,128)(2,1)S(1)}, bf16[64,3584]{1,0:T(8,128)(2,1)S(1)}, u32[]{:S(2)}, u32[]{:S(2)}) collective-permute-start(bf16[64,3584]{1,0:T(8,128)(2,1)S(1)} %get-tuple-element.24), channel_id=1, source_target_pairs={{0,8},{8,0},{1,9},{9,1},{2,10},{10,2},{3,11},{11,3},{4,12},{12,4},... | collective-permute-start | bytes 1376264 | tf_op jit(solution)/shard_map/ppermute | solution.py:150
  28.5 29.9 %copy-start.2 = (f32[1,3584]{1,0:T(1,128)S(1)}, f32[1,3584]{1,0:T(1,128)}, u32[]{:S(2)}) copy-start(f32[1,3584]{1,0:T(1,128)} %avg_ref.1) | copy-start | bytes 43012
  28.5 29.9 %copy-start.3 = (f32[1,3584]{1,0:T(1,128)S(1)}, f32[1,3584]{1,0:T(1,128)}, u32[]{:S(2)}) copy-start(f32[1,3584]{1,0:T(1,128)} %sq_ref.1) | copy-start | bytes 43012
  58.7 28.3 %copy-start.1 = (f32[64,3584]{1,0:T(8,128)S(1)}, f32[64,3584]{1,0:T(8,128)}, u32[]{:S(2)}) copy-start(f32[64,3584]{1,0:T(8,128)} %weight_ref.1) | copy-start | bytes 2752516
